TPU v7x, 32 devices: a whole 2x2x4 slice. The times are simulated.
32 devices in a mesh: rows: 8 (over z, y), chan: 4 (over x, core).
Axes of the slice: x: 2, y: 2, z: 4, core: 2. Of those that a mesh axis runs over, the one named last changes fastest.
Arguments:
- latent: bfloat16 [32, 128, 1280], P('rows', None, 'chan'), may hold values from -6 to 6
- stale_latent: bfloat16 [16, 128, 1280], P('rows', None, 'chan'), may hold values from -6 to 6
- stale_hidden: bfloat16 [16, 128, 1280], P('rows', None, 'chan'), may hold values from -4 to 4
- first_kernel: bfloat16 [3, 3, 1280, 1280], P(None, None, None, 'chan'), may hold values from -0.0546875 to 0.0546875
- second_kernel: bfloat16 [3, 3, 1280, 1280], P(None, None, None, 'chan'), may hold values from -0.0546875 to 0.0546875
- scale_table: float32 [1000, 1280], P(None, 'chan'), may hold values from 0.3 to 3
- timestep: int32 [1], replicated, may hold values from 0 to 999
- cotangent: bfloat16 [32, 128, 1280], P('rows', None, 'chan'), may hold values from -6 to 6
Outputs:
- output: bfloat16 [32, 128, 1280], P('rows', None, 'chan')
- grad_latent: bfloat16 [32, 128, 1280], P('rows', None, 'chan')
- grad_first: float32 [3, 3, 1280, 1280], P(None, None, 'rows', 'chan')
- grad_second: float32 [3, 3, 1280, 1280], P(None, None, 'rows', 'chan')
Inputs may be any that keep to these rules, and one draw needn't show every extreme that they name: `timestep`: selects a row of scale_table.
All inputs are finite; a program needn't handle non-finite values.
Results may differ from a plain program's by a relative error of at most 0.0058.
Values may be sent and summed in bfloat16 or wider, within the bound.
A program may use at most 192 MiB of HBM per device.

v0:
```python
import functools
import jax
import jax.numpy as jnp
from jax import lax
from jax.experimental import pallas as pl
from jax.experimental.pallas import tpu as pltpu
from jax.sharding import PartitionSpec as P

VMEM_BYTES = 48 * 1024 * 1024
PARAMS = pltpu.CompilerParams(vmem_limit_bytes=VMEM_BYTES)


def silu_slope(values):
    logistic = jax.nn.sigmoid(values)
    return logistic * (1.0 + values * (1.0 - logistic))


def moved_columns(values, offset):
    if offset == 0:
        return values
    cols = values.shape[1]
    lane = lax.broadcasted_iota(jnp.int32, values.shape, 1)
    turned = pltpu.roll(values.astype(jnp.float32), (-offset) % cols, 1)
    inside = (lane + offset >= 0) & (lane + offset < cols)
    return jnp.where(inside, turned, 0.0).astype(jnp.bfloat16)


def forward_body(finish, x_ref, k_ref, *refs):
    *others, shifted, total = refs
    step = pl.program_id(0)
    rows, _, cols = x_ref.shape
    inner = rows - 2
    for col_tap in range(3):

        @pl.when(step == 3 * col_tap)
        def _():
            for row in range(rows):
                shifted[:, row * cols : (row + 1) * cols] = moved_columns(x_ref[row], col_tap - 1)

    start = pl.multiple_of(lax.rem(step, 3) * cols, cols)
    product = jnp.dot(
        k_ref[0, 0],
        shifted[:, pl.ds(start, inner * cols)],
        preferred_element_type=jnp.float32,
    )

    @pl.when(step == 0)
    def _():
        total[...] = product

    @pl.when(step > 0)
    def _():
        total[...] += product

    @pl.when(step == 8)
    def _():
        for row in range(inner):
            finish(row, total[:, row * cols : (row + 1) * cols], *others)


def forward_conv(finish, x, kernel, extras, out_shape):
    rows, depth, cols = x.shape
    wide = kernel.shape[2]
    whole = lambda array: pl.BlockSpec(array.shape, lambda t, n=len(array.shape): (0,) * n)
    flops = 2 * 9 * wide * depth * (rows - 2) * cols
    return pl.pallas_call(
        functools.partial(forward_body, finish),
        grid=(9,),
        in_specs=[
            whole(x),
            pl.BlockSpec((1, 1, wide, depth), lambda t: (t % 3, t // 3, 0, 0)),
            *[whole(extra) for extra in extras],
        ],
        out_specs=[whole(out) for out in out_shape],
        out_shape=out_shape,
        scratch_shapes=[
            pltpu.VMEM((depth, rows * cols), jnp.bfloat16),
            pltpu.VMEM((wide, (rows - 2) * cols), jnp.float32),
        ],
        compiler_params=PARAMS,
        cost_estimate=pl.CostEstimate(
            flops=flops, bytes_accessed=2 * (kernel.size + x.size), transcendentals=0
        ),
    )(x, kernel, *extras)


def finish_hidden(row, values, edge_ref, scale_ref, hidden_ref, slope_ref):
    scale = scale_ref[...]
    scaled = values * scale
    logistic = jax.nn.sigmoid(scaled)
    hidden_ref[row + 1] = (scaled * logistic).astype(jnp.bfloat16)
    slope_ref[row] = logistic * (1.0 + scaled * (1.0 - logistic)) * scale
    if row == 0:
        hidden_ref[0] = edge_ref[0]
        hidden_ref[hidden_ref.shape[0] - 1] = edge_ref[1]


def finish_output(row, values, latent_ref, out_ref):
    out_ref[row] = (latent_ref[row].astype(jnp.float32) + values).astype(jnp.bfloat16)


def backward_body(x_ref, k_ref, out_ref, shifted, total):
    step = pl.program_id(0)
    rows, depth, cols = x_ref.shape
    inner = rows - 2

    @pl.when(step == 0)
    def _():
        for col_tap in range(3):
            for row in range(rows):
                shifted[
                    col_tap * depth : (col_tap + 1) * depth, row * cols : (row + 1) * cols
                ] = moved_columns(x_ref[row], 1 - col_tap)

    start = pl.multiple_of((2 - step) * cols, cols)
    product = lax.dot_general(
        k_ref[0].reshape(3 * depth, k_ref.shape[3]),
        shifted[:, pl.ds(start, inner * cols)],
        (((0,), (0,)), ((), ())),
        preferred_element_type=jnp.float32,
    )

    @pl.when(step == 0)
    def _():
        total[...] = product

    @pl.when(step > 0)
    def _():
        total[...] += product

    @pl.when(step == 2)
    def _():
        peers, width = out_ref.shape[0], out_ref.shape[2]
        for peer in range(peers):
            for row in range(inner):
                out_ref[peer, row] = total[
                    peer * width : (peer + 1) * width, row * cols : (row + 1) * cols
                ].astype(jnp.bfloat16)


def backward_conv(x, kernel, peers):
    rows, depth, cols = x.shape
    wide = kernel.shape[3]
    out_shape = jax.ShapeDtypeStruct((peers, rows - 2, wide // peers, cols), jnp.bfloat16)
    return pl.pallas_call(
        backward_body,
        grid=(3,),
        in_specs=[
            pl.BlockSpec(x.shape, lambda t: (0, 0, 0)),
            pl.BlockSpec((1, 3, depth, wide), lambda t: (t, 0, 0, 0)),
        ],
        out_specs=pl.BlockSpec(out_shape.shape, lambda t: (0, 0, 0, 0)),
        out_shape=out_shape,
        scratch_shapes=[
            pltpu.VMEM((3 * depth, rows * cols), jnp.bfloat16),
            pltpu.VMEM((wide, (rows - 2) * cols), jnp.float32),
        ],
        compiler_params=PARAMS,
        cost_estimate=pl.CostEstimate(
            flops=2 * 9 * wide * depth * (rows - 2) * cols,
            bytes_accessed=2 * (kernel.size + x.size),
            transcendentals=0,
        ),
    )(x, kernel)


def weights_body(scale, starts_ref, field_ref, *refs):
    *grads, out_ref, shifted, total = refs
    shares, blocks, share, wide, cols = field_ref.shape
    rows, depth, _ = grads[0].shape
    height = blocks * rows
    edge = jnp.zeros((wide, cols), jnp.bfloat16)
    for tap in range(3):
        shifted[tap, :, 0:cols] = edge
        shifted[tap, :, (height + 1) * cols : (height + 2) * cols] = edge
    for place in range(rows):

        def shift_block(block, carry, place=place):
            piece = field_ref[place // share, block, place % share]
            span = pl.ds(pl.multiple_of((block * rows + place + 1) * cols, cols), cols)
            for tap in range(3):
                shifted[tap, :, span] = moved_columns(piece, tap - 1)
            return carry

        lax.fori_loop(0, blocks, shift_block, 0)
    for at, grad_ref in enumerate(grads):
        flat = jnp.concatenate([grad_ref[row] for row in range(rows)], axis=1)
        for row_tap in range(3):
            span = pl.ds(pl.multiple_of((starts_ref[at] + row_tap) * cols, cols), rows * cols)
            if wide % 16 == 0:
                product = lax.dot_general(
                    shifted[:, :, span].reshape(3 * wide, rows * cols),
                    flat,
                    (((1,), (1,)), ((), ())),
                    preferred_element_type=jnp.float32,
                ).reshape(3, wide, depth)
                total[row_tap] = product if at == 0 else total[row_tap] + product
            else:
                for tap in range(3):
                    product = lax.dot_general(
                        shifted[tap, :, span],
                        flat,
                        (((1,), (1,)), ((), ())),
                        preferred_element_type=jnp.float32,
                    )
                    total[row_tap, tap] = product if at == 0 else total[row_tap, tap] + product
    out_ref[...] = total[...] * scale


def weight_grads(starts, field, grads):
    shares, blocks, share, wide, cols = field.shape
    rows, depth, _ = grads[0].shape
    height = blocks * rows
    out_shape = jax.ShapeDtypeStruct((3, 3, wide, depth), jnp.float32)
    vmem = pl.BlockSpec(memory_space=pltpu.VMEM)
    return pl.pallas_call(
        functools.partial(weights_body, 1.0 / height),
        in_specs=[pl.BlockSpec(memory_space=pltpu.SMEM), vmem, *[vmem for _ in grads]],
        out_specs=vmem,
        out_shape=out_shape,
        scratch_shapes=[
            pltpu.VMEM((3, wide, (height + 2) * cols), jnp.bfloat16),
            pltpu.VMEM(out_shape.shape, jnp.float32),
        ],
        compiler_params=PARAMS,
        cost_estimate=pl.CostEstimate(
            flops=2 * 9 * wide * depth * height * cols,
            bytes_accessed=2 * field.size + 2 * len(grads) * grads[0].size + 4 * 9 * wide * depth,
            transcendentals=0,
        ),
    )(starts, field, *grads)


def cycle_order(peers):
    return list(range(0, peers, 2)) + list(range(1, peers, 2))[::-1]


def ring_blocks(block, axis):
    peers = lax.axis_size(axis)
    order = cycle_order(peers)
    ahead = [(order[i], order[(i + 1) % peers]) for i in range(peers)]
    back = [(j, i) for i, j in ahead]
    blocks = [block]
    left = right = block
    for hop in range(1, peers // 2 + 1):
        left = lax.ppermute(left, axis, ahead)
        blocks.append(left)
        if hop <= (peers - 1) // 2:
            right = lax.ppermute(right, axis, back)
            blocks.append(right)
    return blocks


def ring_starts(axis, rows):
    peers = lax.axis_size(axis)
    order = cycle_order(peers)
    place = [order.index(i) for i in range(peers)]
    at = jnp.asarray(place, jnp.int32)[lax.axis_index(axis)]
    offsets = [0]
    for hop in range(1, peers // 2 + 1):
        offsets.append(-hop)
        if hop <= (peers - 1) // 2:
            offsets.append(hop)
    where = (at + jnp.asarray(offsets, jnp.int32)) % peers
    return jnp.asarray(order, jnp.int32)[where] * rows


def with_rims(shard, axis):
    peers = lax.axis_size(axis)
    up = [(i, i + 1) for i in range(peers - 1)]
    down = [(j, i) for i, j in up]
    before = lax.ppermute(shard[-1:], axis, up)
    after = lax.ppermute(shard[:1], axis, down)
    return jnp.concatenate([before, shard, after], axis=0)


def scatter_sum(blocks, axis):
    peers = lax.axis_size(axis)
    index = lax.axis_index(axis)
    total = lax.dynamic_index_in_dim(blocks, index, 0, keepdims=False).astype(jnp.float32)
    for step in range(1, peers):
        block = lax.dynamic_index_in_dim(blocks, (index + step) % peers, 0, keepdims=False)
        moved = lax.ppermute(block, axis, [(i, (i + step) % peers) for i in range(peers)])
        total = total + moved.astype(jnp.float32)
    return total


def own_channels(field, axis, others):
    peers = lax.axis_size(axis)
    shares = lax.axis_size(others)
    rows, depth, cols = field.shape
    share = rows // shares
    part = lax.dynamic_slice_in_dim(field, lax.axis_index(others) * share, share, axis=0)
    part = part.reshape(share, peers, depth // peers, cols)
    part = jnp.transpose(part, (1, 0, 2, 3))
    part = lax.all_to_all(part, axis, 0, 0, tiled=True)
    return lax.all_gather(part, others, axis=0)


def on_device(
    latent,
    stale_latent,
    stale_hidden,
    first_kernel,
    second_kernel,
    scale_table,
    timestep,
    cotangent,
):
    row_index = lax.axis_index("rows")
    row_devices = lax.axis_size("rows")
    peers = lax.axis_size("chan")
    upright = lambda field: jnp.transpose(field, (0, 2, 1))
    latent, stale_latent, stale_hidden, cotangent = [
        upright(field) for field in (latent, stale_latent, stale_hidden, cotangent)
    ]
    first = jnp.transpose(first_kernel, (0, 1, 3, 2))
    second = jnp.transpose(second_kernel, (0, 1, 3, 2))
    rows, depth, cols = latent.shape
    latent_f = latent.astype(jnp.float32)
    act = jax.nn.silu(latent_f).astype(jnp.bfloat16)
    edge_act = jax.nn.silu(stale_latent.astype(jnp.float32)).astype(jnp.bfloat16)
    present = jnp.stack([row_index > 0, row_index < row_devices - 1])[:, None, None]
    edge_act = jnp.where(present, edge_act, jnp.zeros_like(edge_act))
    edge_hidden = jnp.where(present, stale_hidden, jnp.zeros_like(stale_hidden))
    act_pad = jnp.concatenate([edge_act[:1], act, edge_act[1:]], axis=0)
    act_all = lax.all_gather(act_pad, "chan", axis=1, tiled=True)
    step_scale = lax.dynamic_index_in_dim(scale_table, timestep[0], 0, keepdims=False)
    scale_map = jnp.broadcast_to(step_scale[:, None], (depth, cols))
    starts = ring_starts("rows", rows)

    grad_hidden = scatter_sum(backward_conv(with_rims(cotangent, "rows"), second, peers), "chan")
    hidden_pad, slope = forward_conv(
        finish_hidden,
        act_all,
        first,
        (edge_hidden, scale_map),
        [
            jax.ShapeDtypeStruct((rows + 2, depth, cols), jnp.bfloat16),
            jax.ShapeDtypeStruct((rows, depth, cols), jnp.float32),
        ],
    )
    hidden_all = lax.all_gather(hidden_pad, "chan", axis=1, tiled=True)
    delta = (grad_hidden * slope).astype(jnp.bfloat16)
    grad_pre = scatter_sum(backward_conv(with_rims(delta, "rows"), first, peers), "chan")
    grad_latent = (
        latent_f * 0.0 + cotangent.astype(jnp.float32) + grad_pre * silu_slope(latent_f)
    ).astype(jnp.bfloat16)
    (output,) = forward_conv(
        finish_output,
        hidden_all,
        second,
        (latent,),
        [jax.ShapeDtypeStruct((rows, depth, cols), jnp.bfloat16)],
    )
    act_own = own_channels(act_all[1:-1], "rows", "chan")
    hidden_own = own_channels(hidden_all[1:-1], "rows", "chan")
    grad_first = weight_grads(starts, act_own, ring_blocks(delta, "rows"))
    grad_second = weight_grads(starts, hidden_own, ring_blocks(cotangent, "rows"))
    return (upright(output), upright(grad_latent), grad_first, grad_second)


def solution(mesh):
    in_specs = (
        P("rows", None, "chan"),
        P("rows", None, "chan"),
        P("rows", None, "chan"),
        P(None, None, None, "chan"),
        P(None, None, None, "chan"),
        P(None, "chan"),
        P(),
        P("rows", None, "chan"),
    )
    out_specs = (
        P("rows", None, "chan"),
        P("rows", None, "chan"),
        P(None, None, "rows", "chan"),
        P(None, None, "rows", "chan"),
    )
    return jax.shard_map(
        on_device, mesh=mesh, in_specs=in_specs, out_specs=out_specs, check_vma=False
    )
```

profile of v0, /device:TPU:0, one launch (start us, length us, event | category | flops | bytes accessed | tf_op | source)
XLA Modules:
  0.0 209.4 jit_solution(2195163617641506435)
XLA Ops:
  7.3 1.1 fusion.21
  8.5 1.2 fusion.3
  9.7 0.8 pad_maximum_fusion
  11.2 0.2 dynamic-slice_reduce_fusion
  11.6 23.7 %all-gather.7.cloned.1.call-done.x_ref = bf16[6,1280,128]{2,1,0:T(8,128)(2,1)} async-done(((bf16[6,320,128]{2,1,0:T(8,128)(2,1)}), bf16[6,1280,128]{2,1,0:T(8,128)(2,1)}) %all-gather.7.cloned.1.call-update) | async-done | bytes 1966096 | tf_op jit(solution)/shard_map/all_gather | solution.py:327
  35.2 0.1 broadcast_in_dim.28.refs_1_
  35.3 1.5 copy-done.5
  36.9 11.4 %shard_map.138 = (bf16[6,320,128]{2,1,0:T(8,128)(2,1)}, f32[4,320,128]{2,1,0:T(8,128)S(1)}) custom-call(bf16[6,1280,128]{2,1,0:T(8,128)(2,1)S(1)} %copy-done.5, bf16[3,3,320,1280]{3,2,1,0:T(8,128)(2,1)} %bitcast.67, bf16[2,320,128]{2,1,0:T(8,128)(2,1)S(1)} %select_bitcast_fusion.refs_0_, f32[320,128]{1,0:T(8,128)S(1)} %broadcast_in_dim.28.refs_1_), custom_call_target="tpu_custom_call" | custom-call | flops 3774873600 | bytes 9338880 | tf_op jit(solution)/shard_map/pallas_call | solution.py:66
  48.3 0.8 copy-done.6
  49.2 1.3 slice-done.1
  50.6 16.9 %all_to_all.10 = bf16[8,1,160,128]{3,2,1,0:T(8,128)(2,1)} all-to-all(bf16[8,1,160,128]{3,2,1,0:T(8,128)(2,1)S(1)} %bitcast.66), channel_id=1, replica_groups=mesh['rows'=8,'chan'=4] {'rows'}, dimensions={0} | all-to-all | bytes 655360 | tf_op jit(solution)/shard_map/all_to_all | solution.py:296
  67.5 1.3 collective-permute-start.1
  68.8 4.6 %collective-permute-start = (bf16[1,320,128]{2,1,0:T(8,128)(2,1)S(1)}, bf16[1,320,128]{2,1,0:T(8,128)(2,1)S(1)}, u32[]{:S(2)}, u32[]{:S(2)}) collective-permute-start(bf16[1,320,128]{2,1,0:T(8,128)(2,1)S(1)} %get-tuple-element.16), channel_id=1, source_target_pairs={{0,4},{4,8},{8,12},{12,16},{16,20},{20,24},{24,28},{1,5},{5,9},{9,... | collective-permute-start | bytes 245768 | tf_op jit(solution)/shard_map/ppermute | solution.py:272
  73.4 0.4 collective-permute-done.1
  73.8 1.6 collective-permute-done
  75.5 7.7 %shard_map.140 = bf16[4,4,320,128]{3,2,1,0:T(8,128)(2,1)S(1)} custom-call(bf16[6,320,128]{2,1,0:T(8,128)(2,1)S(1)} %pad_maximum_fusion.1.x_ref, bf16[3,3,320,1280]{3,2,1,0:T(8,128)(2,1)} %bitcast.69), custom_call_target="tpu_custom_call" | custom-call | flops 3774873600 | bytes 7864320 | tf_op jit(solution)/shard_map/pallas_call | solution.py:145
  83.2 1.0 dynamic-slice_bitcast_fusion.5
  84.1 0.5 collective-permute-start.3
  84.6 0.2 collective-permute-start.2
  84.9 3.5 %collective-permute-start.17 = (bf16[4,320,128]{2,1,0:T(8,128)(2,1)S(1)}, bf16[4,320,128]{2,1,0:T(8,128)(2,1)}, u32[]{:S(2)}, u32[]{:S(2)}) collective-permute-start(bf16[4,320,128]{2,1,0:T(8,128)(2,1)S(1)} %bitcast.60), channel_id=1, source_target_pairs={{0,8},{8,16},{16,24},{24,28},{28,20},{20,12},{12,4},{4,0},{1,9},{9... | collective-permute-start | bytes 983048 | tf_op jit(solution)/shard_map/ppermute | solution.py:246
  88.4 1.3 slice-done
  89.7 0.7 constant_dynamic-slice_fusion
  90.5 4.1 %all-to-all-start.1 = ((bf16[8,1,160,128]{3,2,1,0:T(8,128)(2,1)}), bf16[8,1,160,128]{3,2,1,0:T(8,128)(2,1)}, u32[]{:S(2)}, u32[]{:S(2)}) async-start(bf16[8,1,160,128]{3,2,1,0:T(8,128)(2,1)} %bitcast.22), calls=%async_computation.1 | async-start | bytes 655360 | tf_op jit(solution)/shard_map/all_to_all | solution.py:296
  94.6 8.7 %collective-permute-done.3 = bf16[4,320,128]{2,1,0:T(8,128)(2,1)} collective-permute-done((bf16[4,320,128]{2,1,0:T(8,128)(2,1)}, bf16[4,320,128]{2,1,0:T(8,128)(2,1)}, u32[]{:S(2)}, u32[]{:S(2)}) %collective-permute-start.3) | collective-permute-done | bytes 327712 | tf_op jit(solution)/shard_map/ppermute | solution.py:283
  103.3 0.4 collective-permute-done.2
  103.6 1.6 fusion.15.refs_0_
  105.2 1.5 collective-permute-start.10
  106.8 0.6 dynamic_slice.47
  107.4 1.5 collective-permute-start.19
  108.9 0.6 collective-permute-start.11
  109.4 1.3 collective-permute-start.6
  110.8 4.6 %collective-permute-start.5 = (bf16[1,320,128]{2,1,0:T(8,128)(2,1)S(1)}, bf16[1,320,128]{2,1,0:T(8,128)(2,1)S(1)}, u32[]{:S(2)}, u32[]{:S(2)}) collective-permute-start(bf16[1,320,128]{2,1,0:T(8,128)(2,1)S(1)} %get-tuple-element.14), channel_id=1, source_target_pairs={{0,4},{4,8},{8,12},{12,16},{16,20},{20,24},{24,28},{1,5},{5,9},{9,... | collective-permute-start | bytes 245768 | tf_op jit(solution)/shard_map/ppermute | solution.py:272
  115.3 0.6 collective-permute-done.10.refs_1_
  115.9 1.5 collective-permute-start.12
  117.4 0.7 compare_select_fusion
  118.1 4.9 %collective-permute-done.19.refs_3_ = bf16[4,320,128]{2,1,0:T(8,128)(2,1)S(1)} collective-permute-done((bf16[4,320,128]{2,1,0:T(8,128)(2,1)}, bf16[4,320,128]{2,1,0:T(8,128)(2,1)S(1)}, u32[]{:S(2)}, u32[]{:S(2)}) %collective-permute-start.19) | collective-permute-done | bytes 327712 | tf_op jit(solution)/shard_map/ppermute | solution.py:246
  123.0 1.5 collective-permute-start.20
  124.4 0.3 collective-permute-done.6
  124.7 0.3 collective-permute-start.21
  125.1 1.8 collective-permute-start.13
  126.9 5.0 %collective-permute-done.12.refs_3_ = bf16[4,320,128]{2,1,0:T(8,128)(2,1)} collective-permute-done((bf16[4,320,128]{2,1,0:T(8,128)(2,1)S(1)}, bf16[4,320,128]{2,1,0:T(8,128)(2,1)}, u32[]{:S(2)}, u32[]{:S(2)}) %collective-permute-start.12) | collective-permute-done | bytes 327712 | tf_op jit(solution)/shard_map/ppermute | solution.py:246
  131.8 7.6 %shard_map.141 = bf16[4,4,320,128]{3,2,1,0:T(8,128)(2,1)S(1)} custom-call(bf16[6,320,128]{2,1,0:T(8,128)(2,1)S(1)} %pad_maximum_fusion.2.x_ref, bf16[3,3,320,1280]{3,2,1,0:T(8,128)(2,1)} %bitcast.68), custom_call_target="tpu_custom_call" | custom-call | flops 3774873600 | bytes 7864320 | tf_op jit(solution)/shard_map/pallas_call | solution.py:145
  139.5 1.0 copy-done.3
  140.5 1.0 dynamic-slice_bitcast_fusion.2
  141.5 0.4 collective-permute-start.8
  141.9 0.3 copy-done.9
  142.2 0.8 copy-done.11
  143.0 0.5 collective-permute-start.7
  143.5 0.6 gather_fusion
  144.1 2.1 collective-permute-start.15
  146.2 3.7 %collective-permute-done.9 = bf16[4,320,128]{2,1,0:T(8,128)(2,1)} collective-permute-done((bf16[4,320,128]{2,1,0:T(8,128)(2,1)}, bf16[4,320,128]{2,1,0:T(8,128)(2,1)}, u32[]{:S(2)}, u32[]{:S(2)}) %collective-permute-start.9) | collective-permute-done | bytes 327712 | tf_op jit(solution)/shard_map/ppermute | solution.py:283
  149.9 2.0 collective-permute-start.22
  151.9 4.9 %collective-permute-done.8 = bf16[4,320,128]{2,1,0:T(8,128)(2,1)} collective-permute-done((bf16[4,320,128]{2,1,0:T(8,128)(2,1)}, bf16[4,320,128]{2,1,0:T(8,128)(2,1)}, u32[]{:S(2)}, u32[]{:S(2)}) %collective-permute-start.8) | collective-permute-done | bytes 327712 | tf_op jit(solution)/shard_map/ppermute | solution.py:283
  156.8 1.3 collective-permute-start.23
  158.1 2.5 %fusion.20 = bf16[4,128,320]{1,2,0:T(8,128)(2,1)} fusion(bf16[4,320,128]{2,1,0:T(8,128)(2,1)} %collective-permute-done.9, bf16[4,320,128]{2,1,0:T(8,128)(2,1)} %collective-permute-done.8, bf16[4,320,128]{2,1,0:T(8,128)(2,1)} %collective-permute-done.7, bf16[4,4,320,128]{3,2,1,0:T(8,128)(2,1)} %copy-done.3, s32[]{:T(128)S(6)} %select_n.69, ...), kind=kLoop, calls=%fused_computation.38 | loop fusion | flops 3440640 | bytes 2293764 | tf_op jit(solution)/shard_map/transpose | solution.py:313
  160.6 0.7 copy-done.13
  161.3 0.7 copy-done.15
  162.1 1.3 copy-done.7
  163.4 1.0 copy-done.14
  164.4 1.0 copy-done.16
  165.3 12.4 %shard_map.142 = f32[3,3,160,320]{3,2,1,0:T(8,128)} custom-call(s32[8]{0:T(128)S(1)} %broadcast_multiply_fusion.starts_ref, bf16[4,8,1,160,128]{4,3,2,1,0:T(8,128)(2,1)S(1)} %bitcast.64, bf16[4,320,128]{2,1,0:T(8,128)(2,1)S(1)} %fusion.15.refs_0_, bf16[4,320,128]{2,1,0:T(8,128)(2,1)S(1)} %collective-permute-done.10.refs_1_, ...), custom_call_target="tpu_custom_call" | custom-call | flops 3774873600 | bytes 5775360 | tf_op jit(solution)/shard_map/pallas_call | solution.py:216
  177.7 11.2 %shard_map.139 = bf16[4,320,128]{2,1,0:T(8,128)(2,1)} custom-call(bf16[6,1280,128]{2,1,0:T(8,128)(2,1)S(1)} %copy-done.4, bf16[3,3,320,1280]{3,2,1,0:T(8,128)(2,1)} %bitcast.70, bf16[4,320,128]{2,1,0:T(8,128)(2,1)S(1)} %bitcast.63), custom_call_target="tpu_custom_call" | custom-call | flops 3774873600 | bytes 9338880 | tf_op jit(solution)/shard_map/pallas_call | solution.py:66
  189.0 1.3 copy-done.8
  190.3 12.5 %shard_map.143 = f32[3,3,160,320]{3,2,1,0:T(8,128)} custom-call(s32[8]{0:T(128)S(1)} %broadcast_multiply_fusion.starts_ref, bf16[4,8,1,160,128]{4,3,2,1,0:T(8,128)(2,1)S(1)} %bitcast.65, bf16[4,320,128]{2,1,0:T(8,128)(2,1)S(1)} %bitcast.62, bf16[4,320,128]{2,1,0:T(8,128)(2,1)} %collective-permute-done.17.refs_1_, ...), custom_call_target="tpu_custom_call" | custom-call | flops 3774873600 | bytes 5775360 | tf_op jit(solution)/shard_map/pallas_call | solution.py:216
  (76 shorter events, 0.7 us)
Async XLA Ops:
  7.2 4.1 %copy-start = (f32[1000,320]{0,1:T(8,128)S(1)}, f32[1000,320]{0,1:T(8,128)}, u32[]{:S(2)}) copy-start(f32[1000,320]{0,1:T(8,128)} %param.16) | copy-start | bytes 3840004
  7.2 28.0 %all-gather.7.cloned.1.call-start = ((), (), s32[]{:S(2)}) async-start(), calls=%async_computation.2 | async-start | bytes 2457600 | tf_op jit(solution)/shard_map/all_gather | solution.py:327
  8.4 3.0 %copy-start.19 = (bf16[2,128,320]{1,2,0:T(8,128)(2,1)S(1)}, bf16[2,128,320]{1,2,0:T(8,128)(2,1)}, u32[]{:S(2)}) copy-start(bf16[2,128,320]{1,2,0:T(8,128)(2,1)} %param.13) | copy-start | bytes 491524
  10.5 77.9 %all-gather.9.cloned.1.call-start = ((), (), s32[]{:S(2)}) async-start(), calls=%async_computation.3 | async-start | bytes 2457600 | tf_op jit(solution)/shard_map/all_gather | solution.py:343
  35.3 1.6 copy-start.5
  48.3 0.8 copy-start.6
  49.2 112.9 %all-gather.11.cloned.1.call-start = ((), (), s32[]{:S(2)}) async-start(), calls=%async_computation.4 | async-start | bytes 1638400 | tf_op jit(solution)/shard_map/all_gather | solution.py:297
  49.2 1.3 slice-start.1
  50.5 16.9 %copy-start.1 = (bf16[4,128,320]{1,2,0:T(8,128)(2,1)S(1)}, bf16[4,128,320]{1,2,0:T(8,128)(2,1)}, u32[]{:S(2)}) copy-start(bf16[4,128,320]{1,2,0:T(8,128)(2,1)} %param.18) | copy-start | bytes 983044
  67.5 6.3 %collective-permute-start.1 = (bf16[1,320,128]{2,1,0:T(8,128)(2,1)S(1)}, bf16[1,320,128]{2,1,0:T(8,128)(2,1)S(1)}, u32[]{:S(2)}, u32[]{:S(2)}) collective-permute-start(bf16[1,320,128]{2,1,0:T(8,128)(2,1)S(1)} %get-tuple-element.17), channel_id=1, source_target_pairs={{4,0},{8,4},{12,8},{16,12},{20,16},{24,20},{28,24},{5,1},{9,5},{13... | collective-permute-start | bytes 245768 | tf_op jit(solution)/shard_map/ppermute | solution.py:273
  68.8 6.6 %collective-permute-start = (bf16[1,320,128]{2,1,0:T(8,128)(2,1)S(1)}, bf16[1,320,128]{2,1,0:T(8,128)(2,1)S(1)}, u32[]{:S(2)}, u32[]{:S(2)}) collective-permute-start(bf16[1,320,128]{2,1,0:T(8,128)(2,1)S(1)} %get-tuple-element.16), channel_id=1, source_target_pairs={{0,4},{4,8},{8,12},{12,16},{16,20},{20,24},{24,28},{1,5},{5,9},{9,... | collective-permute-start | bytes 245768 | tf_op jit(solution)/shard_map/ppermute | solution.py:272
  84.1 10.5 %collective-permute-start.4 = (bf16[4,320,128]{2,1,0:T(8,128)(2,1)}, bf16[4,320,128]{2,1,0:T(8,128)(2,1)S(1)}, u32[]{:S(2)}, u32[]{:S(2)}) collective-permute-start(bf16[4,320,128]{2,1,0:T(8,128)(2,1)} %get-tuple-element.12), channel_id=1, source_target_pairs={{0,3},{1,0},{2,1},{3,2},{4,7},{5,4},{6,5},{7,6},{8,11},{9,8},{10,9... | collective-permute-start | bytes 983048 | tf_op jit(solution)/shard_map/ppermute | solution.py:283
  84.1 19.1 %collective-permute-start.3 = (bf16[4,320,128]{2,1,0:T(8,128)(2,1)}, bf16[4,320,128]{2,1,0:T(8,128)(2,1)}, u32[]{:S(2)}, u32[]{:S(2)}) collective-permute-start(bf16[4,320,128]{2,1,0:T(8,128)(2,1)} %get-tuple-element.13), channel_id=1, source_target_pairs={{0,2},{1,3},{2,0},{3,1},{4,6},{5,7},{6,4},{7,5},{8,10},{9,11},{10,... | collective-permute-start | bytes 983048 | tf_op jit(solution)/shard_map/ppermute | solution.py:283
  84.6 19.0 %collective-permute-start.2 = (bf16[4,320,128]{2,1,0:T(8,128)(2,1)}, bf16[4,320,128]{2,1,0:T(8,128)(2,1)}, u32[]{:S(2)}, u32[]{:S(2)}) collective-permute-start(bf16[4,320,128]{2,1,0:T(8,128)(2,1)} %get-tuple-element.11), channel_id=1, source_target_pairs={{0,1},{1,2},{2,3},{3,0},{4,5},{5,6},{6,7},{7,4},{8,9},{9,10},{10,1... | collective-permute-start | bytes 983048 | tf_op jit(solution)/shard_map/ppermute | solution.py:283
  84.9 22.5 %collective-permute-start.17 = (bf16[4,320,128]{2,1,0:T(8,128)(2,1)S(1)}, bf16[4,320,128]{2,1,0:T(8,128)(2,1)}, u32[]{:S(2)}, u32[]{:S(2)}) collective-permute-start(bf16[4,320,128]{2,1,0:T(8,128)(2,1)S(1)} %bitcast.60), channel_id=1, source_target_pairs={{0,8},{8,16},{16,24},{24,28},{28,20},{20,12},{12,4},{4,0},{1,9},{9... | collective-permute-start | bytes 983048 | tf_op jit(solution)/shard_map/ppermute | solution.py:246
  88.4 22.4 %collective-permute-start.18 = (bf16[4,320,128]{2,1,0:T(8,128)(2,1)S(1)}, bf16[4,320,128]{2,1,0:T(8,128)(2,1)}, u32[]{:S(2)}, u32[]{:S(2)}) collective-permute-start(bf16[4,320,128]{2,1,0:T(8,128)(2,1)S(1)} %bitcast.61), channel_id=1, source_target_pairs={{8,0},{16,8},{24,16},{28,24},{20,28},{12,20},{4,12},{0,4},{9,1},{1... | collective-permute-start | bytes 983048 | tf_op jit(solution)/shard_map/ppermute | solution.py:249
  88.4 1.3 slice-start
  90.5 20.3 %all-to-all-start.1 = ((bf16[8,1,160,128]{3,2,1,0:T(8,128)(2,1)}), bf16[8,1,160,128]{3,2,1,0:T(8,128)(2,1)}, u32[]{:S(2)}, u32[]{:S(2)}) async-start(bf16[8,1,160,128]{3,2,1,0:T(8,128)(2,1)} %bitcast.22), calls=%async_computation.1 | async-start | bytes 655360 | tf_op jit(solution)/shard_map/all_to_all | solution.py:296
  94.5 12.2 %copy-start.21 = (s32[8]{0:T(128)S(1)}, s32[8]{0:T(128)}, u32[]{:S(2)}) copy-start(s32[8]{0:T(128)} %constant.99.clone) | copy-start | bytes 100
  94.5 94.4 %all-gather.13.cloned.1.call-start = ((), (), s32[]{:S(2)}) async-start(), calls=%async_computation.5 | async-start | bytes 1638400 | tf_op jit(solution)/shard_map/all_gather | solution.py:297
  94.6 9.0 %copy-start.18 = (bf16[4,320,128]{2,1,0:T(8,128)(2,1)}, bf16[4,320,128]{2,1,0:T(8,128)(2,1)S(1)}, u32[]{:S(2)}) copy-start(bf16[4,320,128]{2,1,0:T(8,128)(2,1)S(1)} %collective-permute-done.4) | copy-start | bytes 983044
  103.6 13.8 %copy-start.20 = (s32[8]{0:T(128)S(1)}, s32[8]{0:T(128)}, u32[]{:S(2)}) copy-start(s32[8]{0:T(128)} %constant.100.clone) | copy-start | bytes 100
  105.2 10.7 %collective-permute-start.10 = (bf16[4,320,128]{2,1,0:T(8,128)(2,1)S(1)}, bf16[4,320,128]{2,1,0:T(8,128)(2,1)S(1)}, u32[]{:S(2)}, u32[]{:S(2)}) collective-permute-start(bf16[4,320,128]{2,1,0:T(8,128)(2,1)S(1)} %fusion.15.refs_0_), channel_id=1, source_target_pairs={{0,8},{8,16},{16,24},{24,28},{28,20},{20,12},{12,4},{4,0},{1,9},{9... | collective-permute-start | bytes 983048 | tf_op jit(solution)/shard_map/ppermute | solution.py:246
  107.4 15.6 %collective-permute-start.19 = (bf16[4,320,128]{2,1,0:T(8,128)(2,1)}, bf16[4,320,128]{2,1,0:T(8,128)(2,1)S(1)}, u32[]{:S(2)}, u32[]{:S(2)}) collective-permute-start(bf16[4,320,128]{2,1,0:T(8,128)(2,1)} %collective-permute-done.17.refs_1_), channel_id=1, source_target_pairs={{0,8},{8,16},{16,24},{24,28},{28,20},{20,12},{12,4},{4,0},{1,9},{9... | collective-permute-start | bytes 983048 | tf_op jit(solution)/shard_map/ppermute | solution.py:246
  108.9 16.2 %collective-permute-start.11 = (bf16[4,320,128]{2,1,0:T(8,128)(2,1)S(1)}, bf16[4,320,128]{2,1,0:T(8,128)(2,1)S(1)}, u32[]{:S(2)}, u32[]{:S(2)}) collective-permute-start(bf16[4,320,128]{2,1,0:T(8,128)(2,1)S(1)} %fusion.15.refs_0_), channel_id=1, source_target_pairs={{8,0},{16,8},{24,16},{28,24},{20,28},{12,20},{4,12},{0,4},{9,1},{1... | collective-permute-start | bytes 983048 | tf_op jit(solution)/shard_map/ppermute | solution.py:249
  109.4 15.3 %collective-permute-start.6 = (bf16[1,320,128]{2,1,0:T(8,128)(2,1)S(1)}, bf16[1,320,128]{2,1,0:T(8,128)(2,1)S(1)}, u32[]{:S(2)}, u32[]{:S(2)}) collective-permute-start(bf16[1,320,128]{2,1,0:T(8,128)(2,1)S(1)} %get-tuple-element.15), channel_id=1, source_target_pairs={{4,0},{8,4},{12,8},{16,12},{20,16},{24,20},{28,24},{5,1},{9,5},{13... | collective-permute-start | bytes 245768 | tf_op jit(solution)/shard_map/ppermute | solution.py:273
  110.8 14.2 %collective-permute-start.5 = (bf16[1,320,128]{2,1,0:T(8,128)(2,1)S(1)}, bf16[1,320,128]{2,1,0:T(8,128)(2,1)S(1)}, u32[]{:S(2)}, u32[]{:S(2)}) collective-permute-start(bf16[1,320,128]{2,1,0:T(8,128)(2,1)S(1)} %get-tuple-element.14), channel_id=1, source_target_pairs={{0,4},{4,8},{8,12},{12,16},{16,20},{20,24},{24,28},{1,5},{5,9},{9,... | collective-permute-start | bytes 245768 | tf_op jit(solution)/shard_map/ppermute | solution.py:272
  115.9 15.9 %collective-permute-start.12 = (bf16[4,320,128]{2,1,0:T(8,128)(2,1)S(1)}, bf16[4,320,128]{2,1,0:T(8,128)(2,1)}, u32[]{:S(2)}, u32[]{:S(2)}) collective-permute-start(bf16[4,320,128]{2,1,0:T(8,128)(2,1)S(1)} %collective-permute-done.10.refs_1_), channel_id=1, source_target_pairs={{0,8},{8,16},{16,24},{24,28},{28,20},{20,12},{12,4},{4,0},{1,9},{9... | collective-permute-start | bytes 983048 | tf_op jit(solution)/shard_map/ppermute | solution.py:246
  123.0 18.5 %collective-permute-start.20 = (bf16[4,320,128]{2,1,0:T(8,128)(2,1)}, bf16[4,320,128]{2,1,0:T(8,128)(2,1)S(1)}, u32[]{:S(2)}, u32[]{:S(2)}) collective-permute-start(bf16[4,320,128]{2,1,0:T(8,128)(2,1)} %collective-permute-done.18.refs_2_), channel_id=1, source_target_pairs={{8,0},{16,8},{24,16},{28,24},{20,28},{12,20},{4,12},{0,4},{9,1},{1... | collective-permute-start | bytes 983048 | tf_op jit(solution)/shard_map/ppermute | solution.py:249
  124.7 17.2 %collective-permute-start.21 = (bf16[4,320,128]{2,1,0:T(8,128)(2,1)S(1)}, bf16[4,320,128]{2,1,0:T(8,128)(2,1)S(1)}, u32[]{:S(2)}, u32[]{:S(2)}) collective-permute-start(bf16[4,320,128]{2,1,0:T(8,128)(2,1)S(1)} %collective-permute-done.19.refs_3_), channel_id=1, source_target_pairs={{0,8},{8,16},{16,24},{24,28},{28,20},{20,12},{12,4},{4,0},{1,9},{9... | collective-permute-start | bytes 983048 | tf_op jit(solution)/shard_map/ppermute | solution.py:246
  125.1 19.1 %collective-permute-start.13 = (bf16[4,320,128]{2,1,0:T(8,128)(2,1)S(1)}, bf16[4,320,128]{2,1,0:T(8,128)(2,1)}, u32[]{:S(2)}, u32[]{:S(2)}) collective-permute-start(bf16[4,320,128]{2,1,0:T(8,128)(2,1)S(1)} %collective-permute-done.11.refs_2_), channel_id=1, source_target_pairs={{8,0},{16,8},{24,16},{28,24},{20,28},{12,20},{4,12},{0,4},{9,1},{1... | collective-permute-start | bytes 983048 | tf_op jit(solution)/shard_map/ppermute | solution.py:249
  131.8 14.4 %collective-permute-start.14 = (bf16[4,320,128]{2,1,0:T(8,128)(2,1)}, bf16[4,320,128]{2,1,0:T(8,128)(2,1)}, u32[]{:S(2)}, u32[]{:S(2)}) collective-permute-start(bf16[4,320,128]{2,1,0:T(8,128)(2,1)} %collective-permute-done.12.refs_3_), channel_id=1, source_target_pairs={{0,8},{8,16},{16,24},{24,28},{28,20},{20,12},{12,4},{4,0},{1,9},{9... | collective-permute-start | bytes 983048 | tf_op jit(solution)/shard_map/ppermute | solution.py:246
  139.5 1.1 copy-start.3
  140.5 3.0 %copy-start.17 = (s32[8]{0:T(128)S(1)}, s32[8]{0:T(128)}, u32[]{:S(2)}) copy-start(s32[8]{0:T(128)} %constant.101.clone) | copy-start | bytes 100
  140.5 17.6 %copy-start.2 = (bf16[4,128,320]{1,2,0:T(8,128)(2,1)S(1)}, bf16[4,128,320]{1,2,0:T(8,128)(2,1)}, u32[]{:S(2)}) copy-start(bf16[4,128,320]{1,2,0:T(8,128)(2,1)} %param.11) | copy-start | bytes 983044
  141.5 8.4 %collective-permute-start.9 = (bf16[4,320,128]{2,1,0:T(8,128)(2,1)}, bf16[4,320,128]{2,1,0:T(8,128)(2,1)}, u32[]{:S(2)}, u32[]{:S(2)}) collective-permute-start(bf16[4,320,128]{2,1,0:T(8,128)(2,1)} %get-tuple-element.9), channel_id=1, source_target_pairs={{0,3},{1,0},{2,1},{3,2},{4,7},{5,4},{6,5},{7,6},{8,11},{9,8},{10,9... | collective-permute-start | bytes 983048 | tf_op jit(solution)/shard_map/ppermute | solution.py:283
  141.5 0.7 copy-start.9
  141.5 15.3 %collective-permute-start.8 = (bf16[4,320,128]{2,1,0:T(8,128)(2,1)}, bf16[4,320,128]{2,1,0:T(8,128)(2,1)}, u32[]{:S(2)}, u32[]{:S(2)}) collective-permute-start(bf16[4,320,128]{2,1,0:T(8,128)(2,1)} %get-tuple-element.10), channel_id=1, source_target_pairs={{0,2},{1,3},{2,0},{3,1},{4,6},{5,7},{6,4},{7,5},{8,10},{9,11},{10,... | collective-permute-start | bytes 983048 | tf_op jit(solution)/shard_map/ppermute | solution.py:283
  142.2 0.8 copy-start.11
  143.0 15.2 %collective-permute-start.7 = (bf16[4,320,128]{2,1,0:T(8,128)(2,1)}, bf16[4,320,128]{2,1,0:T(8,128)(2,1)}, u32[]{:S(2)}, u32[]{:S(2)}) collective-permute-start(bf16[4,320,128]{2,1,0:T(8,128)(2,1)} %get-tuple-element.8), channel_id=1, source_target_pairs={{0,1},{1,2},{2,3},{3,0},{4,5},{5,6},{6,7},{7,4},{8,9},{9,10},{10,1... | collective-permute-start | bytes 983048 | tf_op jit(solution)/shard_map/ppermute | solution.py:283
  144.1 16.5 %collective-permute-start.15 = (bf16[4,320,128]{2,1,0:T(8,128)(2,1)}, bf16[4,320,128]{2,1,0:T(8,128)(2,1)S(1)}, u32[]{:S(2)}, u32[]{:S(2)}) collective-permute-start(bf16[4,320,128]{2,1,0:T(8,128)(2,1)} %collective-permute-done.13.refs_4_), channel_id=1, source_target_pairs={{8,0},{16,8},{24,16},{28,24},{20,28},{12,20},{4,12},{0,4},{9,1},{1... | collective-permute-start | bytes 983048 | tf_op jit(solution)/shard_map/ppermute | solution.py:249
  146.2 15.1 %collective-permute-start.16 = (bf16[4,320,128]{2,1,0:T(8,128)(2,1)}, bf16[4,320,128]{2,1,0:T(8,128)(2,1)S(1)}, u32[]{:S(2)}, u32[]{:S(2)}) collective-permute-start(bf16[4,320,128]{2,1,0:T(8,128)(2,1)} %collective-permute-done.14.refs_5_), channel_id=1, source_target_pairs={{0,8},{8,16},{16,24},{24,28},{28,20},{20,12},{12,4},{4,0},{1,9},{9... | collective-permute-start | bytes 983048 | tf_op jit(solution)/shard_map/ppermute | solution.py:246
  149.9 39.0 %collective-permute-start.22 = (bf16[4,320,128]{2,1,0:T(8,128)(2,1)}, bf16[4,320,128]{2,1,0:T(8,128)(2,1)}, u32[]{:S(2)}, u32[]{:S(2)}) collective-permute-start(bf16[4,320,128]{2,1,0:T(8,128)(2,1)} %copy-done.9), channel_id=1, source_target_pairs={{8,0},{16,8},{24,16},{28,24},{20,28},{12,20},{4,12},{0,4},{9,1},{1... | collective-permute-start | bytes 983048 | tf_op jit(solution)/shard_map/ppermute | solution.py:249
  156.8 32.2 %collective-permute-start.23 = (bf16[4,320,128]{2,1,0:T(8,128)(2,1)}, bf16[4,320,128]{2,1,0:T(8,128)(2,1)}, u32[]{:S(2)}, u32[]{:S(2)}) collective-permute-start(bf16[4,320,128]{2,1,0:T(8,128)(2,1)} %copy-done.11), channel_id=1, source_target_pairs={{0,8},{8,16},{16,24},{24,28},{28,20},{20,12},{12,4},{4,0},{1,9},{9... | collective-permute-start | bytes 983048 | tf_op jit(solution)/shard_map/ppermute | solution.py:246
  160.6 0.7 copy-start.13
  161.3 0.7 copy-start.15
  162.1 1.3 copy-start.7
  163.4 1.0 copy-start.14
  164.4 1.0 copy-start.16
  165.3 12.4 %copy-start.4 = (bf16[6,1280,128]{2,1,0:T(8,128)(2,1)S(1)}, bf16[6,1280,128]{2,1,0:T(8,128)(2,1)}, u32[]{:S(2)}) copy-start(bf16[6,1280,128]{2,1,0:T(8,128)(2,1)} %all-gather.9.cloned.1.call-done.x_ref) | copy-start | bytes 5898244
  177.7 11.3 %copy-start.10 = (bf16[4,320,128]{2,1,0:T(8,128)(2,1)S(1)}, bf16[4,320,128]{2,1,0:T(8,128)(2,1)}, u32[]{:S(2)}) copy-start(bf16[4,320,128]{2,1,0:T(8,128)(2,1)} %copy-done.9) | copy-start | bytes 983044
  177.7 11.3 %copy-start.12 = (bf16[4,320,128]{2,1,0:T(8,128)(2,1)S(1)}, bf16[4,320,128]{2,1,0:T(8,128)(2,1)}, u32[]{:S(2)}) copy-start(bf16[4,320,128]{2,1,0:T(8,128)(2,1)} %copy-done.11) | copy-start | bytes 983044
  189.0 1.3 copy-start.8
Sparse Core Ops, SparseCore 0:
  10.6 24.5 all-gather.6
  49.3 21.8 all-gather.8
  72.8 21.1 all-gather.10
  110.9 19.3 all-gather.12
where the time goes:
time: 212 us; the launch traced here: 209 us
  Pallas kernels  62.9 us (30%)
  waiting for transfers between devices  54.1 us (26%)
  starting transfers between devices  35.1 us (17%)
  local copies, waits for them, and re-layouts  17.5 us (8%)
  blocking collectives  16.9 us (8%)
  between operations  14.8 us (7%)
  other arithmetic  8.14 us (4%)
    pallas_call x2, Pallas kernels, weight_grads(): pl.pallas_call(functools.partial(weights_body, 1.0 / height), in_specs=[p...  24.9 us
    all_gather x1, waiting for transfers between devices, on_device(): act_all = lax.all_gather(act_pad, 'chan', axis=1, tiled=True)  23.7 us
    pallas_call x2, Pallas kernels, forward_conv(): pl.pallas_call(functools.partial(forward_body, finish), grid=(9,), in_spe...  22.7 us
    ppermute x6, waiting for transfers between devices, scatter_sum(): lax.ppermute(block, axis, [(i, (i + step) % peers) for i in range(peers)])  17.6 us
    all_to_all x1, blocking collectives, own_channels(): part = lax.all_to_all(part, axis, 0, 0, tiled=True)  16.9 us
    pallas_call x2, Pallas kernels, backward_conv(): pl.pallas_call(backward_body, grid=(3,), in_specs=[pl.BlockSpec(x.shape,...  15.3 us
    unnamed x44, local copies, waits for them, and re-layouts  10.6 us
    ppermute x8, waiting for transfers between devices, ring_blocks(): left = lax.ppermute(left, axis, ahead)  10.4 us
  transfers between devices with their start and end apart: 29, of which 11 were waited for; matrix products, arithmetic and copies ran while one was open for 4% of the time, Pallas kernels for 19%

commit v1 on v0

--- a/solution.py
+++ b/solution.py
@@ -25,22 +25,29 @@
     return jnp.where(inside, turned, 0.0).astype(jnp.bfloat16)
 
 
+def shifted_sums(values, offset):
+    cols = values.shape[1]
+    lane = lax.broadcasted_iota(jnp.int32, values.shape, 1)
+    inside = (lane + offset >= 0) & (lane + offset < cols)
+    return jnp.where(inside, pltpu.roll(values, (-offset) % cols, 1), 0.0)
+
+
 def forward_body(finish, x_ref, k_ref, *refs):
-    *others, shifted, total = refs
+    *others, flat, total = refs
     step = pl.program_id(0)
     rows, _, cols = x_ref.shape
     inner = rows - 2
-    for col_tap in range(3):
-
-        @pl.when(step == 3 * col_tap)
-        def _():
-            for row in range(rows):
-                shifted[:, row * cols : (row + 1) * cols] = moved_columns(x_ref[row], col_tap - 1)
-
-    start = pl.multiple_of(lax.rem(step, 3) * cols, cols)
+    wide = k_ref.shape[2]
+
+    @pl.when(step == 0)
+    def _():
+        for row in range(rows):
+            flat[:, row * cols : (row + 1) * cols] = x_ref[row]
+
+    start = pl.multiple_of(step * cols, cols)
     product = jnp.dot(
-        k_ref[0, 0],
-        shifted[:, pl.ds(start, inner * cols)],
+        k_ref[0].reshape(3 * wide, k_ref.shape[3]),
+        flat[:, pl.ds(start, inner * cols)],
         preferred_element_type=jnp.float32,
     )
 
@@ -52,10 +59,15 @@
     def _():
         total[...] += product
 
-    @pl.when(step == 8)
+    @pl.when(step == 2)
     def _():
         for row in range(inner):
-            finish(row, total[:, row * cols : (row + 1) * cols], *others)
+            left, middle, right = [
+                total[tap * wide : (tap + 1) * wide, row * cols : (row + 1) * cols]
+                for tap in range(3)
+            ]
+            sums = middle + shifted_sums(left, -1) + shifted_sums(right, 1)
+            finish(row, sums, *others)
 
 
 def forward_conv(finish, x, kernel, extras, out_shape):
@@ -65,17 +77,17 @@
     flops = 2 * 9 * wide * depth * (rows - 2) * cols
     return pl.pallas_call(
         functools.partial(forward_body, finish),
-        grid=(9,),
+        grid=(3,),
         in_specs=[
             whole(x),
-            pl.BlockSpec((1, 1, wide, depth), lambda t: (t % 3, t // 3, 0, 0)),
+            pl.BlockSpec((1, 3, wide, depth), lambda t: (t, 0, 0, 0)),
             *[whole(extra) for extra in extras],
         ],
         out_specs=[whole(out) for out in out_shape],
         out_shape=out_shape,
         scratch_shapes=[
             pltpu.VMEM((depth, rows * cols), jnp.bfloat16),
-            pltpu.VMEM((wide, (rows - 2) * cols), jnp.float32),
+            pltpu.VMEM((3 * wide, (rows - 2) * cols), jnp.float32),
         ],
         compiler_params=PARAMS,
         cost_estimate=pl.CostEstimate(
@@ -185,20 +197,24 @@
         lax.fori_loop(0, blocks, shift_block, 0)
     for at, grad_ref in enumerate(grads):
         flat = jnp.concatenate([grad_ref[row] for row in range(rows)], axis=1)
-        for row_tap in range(3):
-            span = pl.ds(pl.multiple_of((starts_ref[at] + row_tap) * cols, cols), rows * cols)
-            if wide % 16 == 0:
-                product = lax.dot_general(
-                    shifted[:, :, span].reshape(3 * wide, rows * cols),
-                    flat,
-                    (((1,), (1,)), ((), ())),
-                    preferred_element_type=jnp.float32,
-                ).reshape(3, wide, depth)
-                total[row_tap] = product if at == 0 else total[row_tap] + product
-            else:
+        spans = [
+            pl.ds(pl.multiple_of((starts_ref[at] + row_tap) * cols, cols), rows * cols)
+            for row_tap in range(3)
+        ]
+        if wide % 16 == 0:
+            windows = [shifted[:, :, span].reshape(3 * wide, rows * cols) for span in spans]
+            product = lax.dot_general(
+                jnp.concatenate(windows, axis=0),
+                flat,
+                (((1,), (1,)), ((), ())),
+                preferred_element_type=jnp.float32,
+            ).reshape(3, 3, wide, depth)
+            total[...] = product if at == 0 else total[...] + product
+        else:
+            for row_tap in range(3):
                 for tap in range(3):
                     product = lax.dot_general(
-                        shifted[tap, :, span],
+                        shifted[tap, :, spans[row_tap]],
                         flat,
                         (((1,), (1,)), ((), ())),
                         preferred_element_type=jnp.float32,
@@ -274,15 +290,19 @@
     return jnp.concatenate([before, shard, after], axis=0)
 
 
-def scatter_sum(blocks, axis):
+def scatter_sum(blocks, axis, before=None):
     peers = lax.axis_size(axis)
     index = lax.axis_index(axis)
-    total = lax.dynamic_index_in_dim(blocks, index, 0, keepdims=False).astype(jnp.float32)
+    own = lax.dynamic_index_in_dim(blocks, index, 0, keepdims=False)
+    moved = []
     for step in range(1, peers):
         block = lax.dynamic_index_in_dim(blocks, (index + step) % peers, 0, keepdims=False)
-        moved = lax.ppermute(block, axis, [(i, (i + step) % peers) for i in range(peers)])
-        total = total + moved.astype(jnp.float32)
-    return total
+        moved.append(lax.ppermute(block, axis, [(i, (i + step) % peers) for i in range(peers)]))
+    own, before = lax.optimization_barrier((own, before))
+    total = own.astype(jnp.float32)
+    for block in moved:
+        total = total + block.astype(jnp.float32)
+    return total, before
 
 
 def own_channels(field, axis, others):
@@ -329,10 +349,14 @@
     scale_map = jnp.broadcast_to(step_scale[:, None], (depth, cols))
     starts = ring_starts("rows", rows)
 
-    grad_hidden = scatter_sum(backward_conv(with_rims(cotangent, "rows"), second, peers), "chan")
+    cotangent_pad, ring_cotangent = lax.optimization_barrier(
+        (with_rims(cotangent, "rows"), cotangent)
+    )
+    partial = backward_conv(cotangent_pad, second, peers)
+    act_ready, partial = lax.optimization_barrier((act_all, partial))
     hidden_pad, slope = forward_conv(
         finish_hidden,
-        act_all,
+        act_ready,
         first,
         (edge_hidden, scale_map),
         [
@@ -340,23 +364,28 @@
             jax.ShapeDtypeStruct((rows, depth, cols), jnp.float32),
         ],
     )
+    grad_hidden, slope = scatter_sum(partial, "chan", slope)
     hidden_all = lax.all_gather(hidden_pad, "chan", axis=1, tiled=True)
     delta = (grad_hidden * slope).astype(jnp.bfloat16)
-    grad_pre = scatter_sum(backward_conv(with_rims(delta, "rows"), first, peers), "chan")
+    delta_pad = with_rims(delta, "rows")
+    delta_pad, ring_delta = lax.optimization_barrier((delta_pad, delta))
+    partial = backward_conv(delta_pad, first, peers)
+    hidden_ready, act_ready, partial = lax.optimization_barrier((hidden_all, act_ready, partial))
+    hidden_own = own_channels(hidden_ready[1:-1], "rows", "chan")
+    (output,) = forward_conv(
+        finish_output,
+        hidden_ready,
+        second,
+        (latent,),
+        [jax.ShapeDtypeStruct((rows, depth, cols), jnp.bfloat16)],
+    )
+    grad_pre, output = scatter_sum(partial, "chan", output)
     grad_latent = (
         latent_f * 0.0 + cotangent.astype(jnp.float32) + grad_pre * silu_slope(latent_f)
     ).astype(jnp.bfloat16)
-    (output,) = forward_conv(
-        finish_output,
-        hidden_all,
-        second,
-        (latent,),
-        [jax.ShapeDtypeStruct((rows, depth, cols), jnp.bfloat16)],
-    )
     act_own = own_channels(act_all[1:-1], "rows", "chan")
-    hidden_own = own_channels(hidden_all[1:-1], "rows", "chan")
-    grad_first = weight_grads(starts, act_own, ring_blocks(delta, "rows"))
-    grad_second = weight_grads(starts, hidden_own, ring_blocks(cotangent, "rows"))
+    grad_first = weight_grads(starts, act_own, ring_blocks(ring_delta, "rows"))
+    grad_second = weight_grads(starts, hidden_own, ring_blocks(ring_cotangent, "rows"))
     return (upright(output), upright(grad_latent), grad_first, grad_second)
 
 

time: 212 us -> 216 us (1.019)
  waiting for transfers between devices: 54.1 us -> 76.4 us
  blocking collectives: 16.9 us -> 0 us
  starting transfers between devices: 35.1 us -> 47.5 us
  Pallas kernels: 62.9 us -> 57 us
  local copies, waits for them, and re-layouts: 17.5 us -> 12.3 us
    ppermute x8, waiting for transfers between devices: 10.4 us -> 34.4 us  [ring_blocks(): left = lax.ppermute(left, axis, ahead)]
    all_to_all x1 -> x0, blocking collectives: 16.9 us -> none  [own_channels(): part = lax.all_to_all(part, axis, 0, 0, tiled=True)]
    all_gather x1, waiting for transfers between devices: 23.7 us -> 7.26 us  [on_device(): act_all = lax.all_gather(act_pad, 'chan', axis=1, tiled=True)]
    ppermute x8, starting transfers between devices: 9.69 us -> 18.5 us  [ring_blocks(): left = lax.ppermute(left, axis, ahead)]
    all_to_all x1 -> x2, starting transfers between devices: 4.06 us -> 12.8 us  [own_channels(): part = lax.all_to_all(part, axis, 0, 0, tiled=True)]
    all_to_all x1 -> x2, waiting for transfers between devices: 0.01 us -> 8.12 us  [own_channels(): part = lax.all_to_all(part, axis, 0, 0, tiled=True)]
    ppermute x6, starting transfers between devices: 7.95 us -> 0.74 us  [ring_blocks(): right = lax.ppermute(right, axis, back)]
    pallas_call x2, Pallas kernels: 22.7 us -> 16.1 us  [forward_conv(): pl.pallas_call(functools.partial(forward_body, finish), grid=(3,), in_spe...]
  transfers between devices with their start and end apart: 29 -> 30, of which waited for: 11 -> 16; matrix products, arithmetic and copies ran while one was open for 4% -> 3% of each run, Pallas kernels for 19% -> 17%
where the time goes in v1:
time: 216 us; the launch traced here: 215 us
  waiting for transfers between devices  76.4 us (35%)
  Pallas kernels  57 us (26%)
  starting transfers between devices  47.5 us (22%)
  between operations  14.8 us (7%)
  local copies, waits for them, and re-layouts  12.3 us (6%)
  other arithmetic  6.59 us (3%)
    ppermute x8, waiting for transfers between devices, ring_blocks(): left = lax.ppermute(left, axis, ahead)  34.4 us
    pallas_call x2, Pallas kernels, weight_grads(): pl.pallas_call(functools.partial(weights_body, 1.0 / height), in_specs=[p...  25.3 us
    ppermute x6, waiting for transfers between devices, scatter_sum(): lax.ppermute(block, axis, [(i, (i + step) % peers) for i in range(peers)])  22.9 us
    ppermute x8, starting transfers between devices, ring_blocks(): left = lax.ppermute(left, axis, ahead)  18.5 us
    pallas_call x2, Pallas kernels, forward_conv(): pl.pallas_call(functools.partial(forward_body, finish), grid=(3,), in_spe...  16.1 us
    pallas_call x2, Pallas kernels, backward_conv(): pl.pallas_call(backward_body, grid=(3,), in_specs=[pl.BlockSpec(x.shape,...  15.6 us
    all_to_all x2, starting transfers between devices, own_channels(): part = lax.all_to_all(part, axis, 0, 0, tiled=True)  12.8 us
    ppermute x2, starting transfers between devices, with_rims(): before = lax.ppermute(shard[-1:], axis, up)  10.1 us
  transfers between devices with their start and end apart: 30, of which 16 were waited for; matrix products, arithmetic and copies ran while one was open for 3% of the time, Pallas kernels for 17%

profile of v1, /device:TPU:0, one launch (start us, length us, event | category | flops | bytes accessed | tf_op | source)
XLA Modules:
  0.0 214.6 jit_solution(3838971012031673802)
XLA Ops:
  7.2 0.1 pad_add_fusion
  7.3 1.1 fusion.15
  8.5 1.2 fusion.3
  9.7 0.8 pad_maximum_fusion
  10.6 1.3 collective-permute-start.1
  11.9 5.5 %collective-permute-start = (bf16[1,320,128]{2,1,0:T(8,128)(2,1)S(1)}, bf16[1,320,128]{2,1,0:T(8,128)(2,1)S(1)}, u32[]{:S(2)}, u32[]{:S(2)}) collective-permute-start(bf16[1,320,128]{2,1,0:T(8,128)(2,1)S(1)} %get-tuple-element.42), channel_id=1, source_target_pairs={{0,4},{4,8},{8,12},{12,16},{16,20},{20,24},{24,28},{1,5},{5,9},{9,... | collective-permute-start | bytes 245768 | tf_op jit(solution)/shard_map/ppermute | solution.py:288
  17.5 0.1 select_bitcast_fusion.refs_0_
  18.2 0.2 dynamic-slice_reduce_fusion
  18.4 1.6 collective-permute-done
  20.1 7.9 %shard_map.138 = bf16[4,4,320,128]{3,2,1,0:T(8,128)(2,1)S(1)} custom-call(bf16[6,320,128]{2,1,0:T(8,128)(2,1)S(1)} %pad_maximum_fusion.1.x_ref, bf16[3,3,320,1280]{3,2,1,0:T(8,128)(2,1)} %bitcast.65), custom_call_target="tpu_custom_call" | custom-call | flops 3774873600 | bytes 7864320 | tf_op jit(solution)/shard_map/pallas_call | solution.py:157
  28.0 7.3 %all-gather.7.cloned.1.call-done.x_ref = bf16[6,1280,128]{2,1,0:T(8,128)(2,1)} async-done(((bf16[6,320,128]{2,1,0:T(8,128)(2,1)}), bf16[6,1280,128]{2,1,0:T(8,128)(2,1)}) %all-gather.7.cloned.1.call-update) | async-done | bytes 1966096 | tf_op jit(solution)/shard_map/all_gather | solution.py:347
  35.3 0.1 broadcast_in_dim.28.refs_1_
  35.4 1.5 copy-done.4
  36.9 8.1 %shard_map.139 = (bf16[6,320,128]{2,1,0:T(8,128)(2,1)}, f32[4,320,128]{2,1,0:T(8,128)S(1)}) custom-call(bf16[6,1280,128]{2,1,0:T(8,128)(2,1)S(1)} %copy-done.4, bf16[3,3,320,1280]{3,2,1,0:T(8,128)(2,1)} %bitcast.63, bf16[2,320,128]{2,1,0:T(8,128)(2,1)S(1)} %select_bitcast_fusion.refs_0_, f32[320,128]{1,0:T(8,128)S(1)} %broadcast_in_dim.28.refs_1_), custom_call_target="tpu_custom_call" | custom-call | flops 3774873600 | bytes 9338880 | tf_op jit(solution)/shard_map/pallas_call | solution.py:78
  45.0 0.8 copy-done.5
  45.9 1.3 slice-done.1
  47.2 0.8 constant_dynamic-slice_fusion.1
  47.9 5.5 %all-to-all-start = ((bf16[8,1,160,128]{3,2,1,0:T(8,128)(2,1)}), bf16[8,1,160,128]{3,2,1,0:T(8,128)(2,1)}, u32[]{:S(2)}, u32[]{:S(2)}) async-start(bf16[8,1,160,128]{3,2,1,0:T(8,128)(2,1)} %bitcast.20), calls=%async_computation | async-start | bytes 655360 | tf_op jit(solution)/shard_map/all_to_all | solution.py:316
  53.6 1.0 dynamic-slice_bitcast_fusion.6
  54.5 0.1 collective-permute-start.4
  54.7 1.5 collective-permute-start.3
  56.1 8.1 %all-to-all-done = bf16[8,1,160,128]{3,2,1,0:T(8,128)(2,1)} async-done(((bf16[8,1,160,128]{3,2,1,0:T(8,128)(2,1)}), bf16[8,1,160,128]{3,2,1,0:T(8,128)(2,1)}, u32[]{:S(2)}, u32[]{:S(2)}) %all-to-all-start) | async-done | bytes 327712 | tf_op jit(solution)/shard_map/all_to_all | solution.py:316
  64.3 5.8 %collective-permute-done.4 = bf16[4,320,128]{2,1,0:T(8,128)(2,1)S(1)} collective-permute-done((bf16[4,320,128]{2,1,0:T(8,128)(2,1)}, bf16[4,320,128]{2,1,0:T(8,128)(2,1)S(1)}, u32[]{:S(2)}, u32[]{:S(2)}) %collective-permute-start.4) | collective-permute-done | bytes 327712 | tf_op jit(solution)/shard_map/ppermute | solution.py:300
  70.0 10.4 %collective-permute-done.3 = bf16[4,320,128]{2,1,0:T(8,128)(2,1)S(1)} collective-permute-done((bf16[4,320,128]{2,1,0:T(8,128)(2,1)}, bf16[4,320,128]{2,1,0:T(8,128)(2,1)S(1)}, u32[]{:S(2)}, u32[]{:S(2)}) %collective-permute-start.3) | collective-permute-done | bytes 327712 | tf_op jit(solution)/shard_map/ppermute | solution.py:300
  80.4 1.3 multiply_convert_fusion.refs_0_
  81.7 1.3 collective-permute-start.6
  83.0 4.6 %collective-permute-start.5 = (bf16[1,320,128]{2,1,0:T(8,128)(2,1)S(1)}, bf16[1,320,128]{2,1,0:T(8,128)(2,1)S(1)}, u32[]{:S(2)}, u32[]{:S(2)}) collective-permute-start(bf16[1,320,128]{2,1,0:T(8,128)(2,1)S(1)} %get-tuple-element.40), channel_id=1, source_target_pairs={{0,4},{4,8},{8,12},{12,16},{16,20},{20,24},{24,28},{1,5},{5,9},{9,... | collective-permute-start | bytes 245768 | tf_op jit(solution)/shard_map/ppermute | solution.py:288
  87.6 0.5 collective-permute-done.6
  88.1 1.6 collective-permute-done.5
  89.7 7.6 %shard_map.140 = bf16[4,4,320,128]{3,2,1,0:T(8,128)(2,1)S(1)} custom-call(bf16[6,320,128]{2,1,0:T(8,128)(2,1)S(1)} %pad_maximum_fusion.2.x_ref, bf16[3,3,320,1280]{3,2,1,0:T(8,128)(2,1)} %bitcast.64), custom_call_target="tpu_custom_call" | custom-call | flops 3774873600 | bytes 7864320 | tf_op jit(solution)/shard_map/pallas_call | solution.py:157
  97.4 1.3 slice-done
  98.7 0.7 constant_dynamic-slice_fusion
  99.4 7.3 %all-to-all-start.1 = ((bf16[8,1,160,128]{3,2,1,0:T(8,128)(2,1)}), bf16[8,1,160,128]{3,2,1,0:T(8,128)(2,1)}, u32[]{:S(2)}, u32[]{:S(2)}) async-start(bf16[8,1,160,128]{3,2,1,0:T(8,128)(2,1)} %bitcast.62), calls=%async_computation.1 | async-start | bytes 655360 | tf_op jit(solution)/shard_map/all_to_all | solution.py:316
  106.8 2.0 collective-permute-start.10
  108.8 1.5 collective-permute-start.17
  110.2 0.6 collective-permute-start.11
  110.8 9.6 %collective-permute-done.10.refs_1_ = bf16[4,320,128]{2,1,0:T(8,128)(2,1)} collective-permute-done((bf16[4,320,128]{2,1,0:T(8,128)(2,1)S(1)}, bf16[4,320,128]{2,1,0:T(8,128)(2,1)}, u32[]{:S(2)}, u32[]{:S(2)}) %collective-permute-start.10) | collective-permute-done | bytes 327712 | tf_op jit(solution)/shard_map/ppermute | solution.py:262
  120.4 2.6 %collective-permute-start.12 = (bf16[4,320,128]{2,1,0:T(8,128)(2,1)}, bf16[4,320,128]{2,1,0:T(8,128)(2,1)}, u32[]{:S(2)}, u32[]{:S(2)}) collective-permute-start(bf16[4,320,128]{2,1,0:T(8,128)(2,1)} %collective-permute-done.10.refs_1_), channel_id=1, source_target_pairs={{0,8},{8,16},{16,24},{24,28},{28,20},{20,12},{12,4},{4,0},{1,9},{9... | collective-permute-start | bytes 983048 | tf_op jit(solution)/shard_map/ppermute | solution.py:262
  123.1 4.3 %collective-permute-done.17.refs_1_ = bf16[4,320,128]{2,1,0:T(8,128)(2,1)} collective-permute-done((bf16[4,320,128]{2,1,0:T(8,128)(2,1)S(1)}, bf16[4,320,128]{2,1,0:T(8,128)(2,1)}, u32[]{:S(2)}, u32[]{:S(2)}) %collective-permute-start.17) | collective-permute-done | bytes 327712 | tf_op jit(solution)/shard_map/ppermute | solution.py:262
  127.4 2.6 %collective-permute-start.19 = (bf16[4,320,128]{2,1,0:T(8,128)(2,1)}, bf16[4,320,128]{2,1,0:T(8,128)(2,1)}, u32[]{:S(2)}, u32[]{:S(2)}) collective-permute-start(bf16[4,320,128]{2,1,0:T(8,128)(2,1)} %collective-permute-done.17.refs_1_), channel_id=1, source_target_pairs={{0,8},{8,16},{16,24},{24,28},{28,20},{20,12},{12,4},{4,0},{1,9},{9... | collective-permute-start | bytes 983048 | tf_op jit(solution)/shard_map/ppermute | solution.py:262
  130.0 4.5 %collective-permute-done.12.refs_3_ = bf16[4,320,128]{2,1,0:T(8,128)(2,1)} collective-permute-done((bf16[4,320,128]{2,1,0:T(8,128)(2,1)}, bf16[4,320,128]{2,1,0:T(8,128)(2,1)}, u32[]{:S(2)}, u32[]{:S(2)}) %collective-permute-start.12) | collective-permute-done | bytes 327712 | tf_op jit(solution)/shard_map/ppermute | solution.py:262
  134.5 2.5 %collective-permute-start.14 = (bf16[4,320,128]{2,1,0:T(8,128)(2,1)}, bf16[4,320,128]{2,1,0:T(8,128)(2,1)}, u32[]{:S(2)}, u32[]{:S(2)}) collective-permute-start(bf16[4,320,128]{2,1,0:T(8,128)(2,1)} %collective-permute-done.12.refs_3_), channel_id=1, source_target_pairs={{0,8},{8,16},{16,24},{24,28},{28,20},{20,12},{12,4},{4,0},{1,9},{9... | collective-permute-start | bytes 983048 | tf_op jit(solution)/shard_map/ppermute | solution.py:262
  137.0 0.6 dynamic_slice.47
  137.6 0.7 compare_select_fusion
  138.3 3.2 %collective-permute-done.19.refs_3_ = bf16[4,320,128]{2,1,0:T(8,128)(2,1)} collective-permute-done((bf16[4,320,128]{2,1,0:T(8,128)(2,1)}, bf16[4,320,128]{2,1,0:T(8,128)(2,1)}, u32[]{:S(2)}, u32[]{:S(2)}) %collective-permute-start.19) | collective-permute-done | bytes 327712 | tf_op jit(solution)/shard_map/ppermute | solution.py:262
  141.6 2.5 %collective-permute-start.21 = (bf16[4,320,128]{2,1,0:T(8,128)(2,1)}, bf16[4,320,128]{2,1,0:T(8,128)(2,1)}, u32[]{:S(2)}, u32[]{:S(2)}) collective-permute-start(bf16[4,320,128]{2,1,0:T(8,128)(2,1)} %collective-permute-done.19.refs_3_), channel_id=1, source_target_pairs={{0,8},{8,16},{16,24},{24,28},{28,20},{20,12},{12,4},{4,0},{1,9},{9... | collective-permute-start | bytes 983048 | tf_op jit(solution)/shard_map/ppermute | solution.py:262
  144.0 4.5 %collective-permute-done.14.refs_5_ = bf16[4,320,128]{2,1,0:T(8,128)(2,1)} collective-permute-done((bf16[4,320,128]{2,1,0:T(8,128)(2,1)}, bf16[4,320,128]{2,1,0:T(8,128)(2,1)}, u32[]{:S(2)}, u32[]{:S(2)}) %collective-permute-start.14) | collective-permute-done | bytes 327712 | tf_op jit(solution)/shard_map/ppermute | solution.py:262
  148.6 2.5 %collective-permute-start.16 = (bf16[4,320,128]{2,1,0:T(8,128)(2,1)}, bf16[4,320,128]{2,1,0:T(8,128)(2,1)}, u32[]{:S(2)}, u32[]{:S(2)}) collective-permute-start(bf16[4,320,128]{2,1,0:T(8,128)(2,1)} %collective-permute-done.14.refs_5_), channel_id=1, source_target_pairs={{0,8},{8,16},{16,24},{24,28},{28,20},{20,12},{12,4},{4,0},{1,9},{9... | collective-permute-start | bytes 983048 | tf_op jit(solution)/shard_map/ppermute | solution.py:262
  151.1 0.6 gather_fusion
  151.8 3.8 %collective-permute-done.21.refs_5_ = bf16[4,320,128]{2,1,0:T(8,128)(2,1)} collective-permute-done((bf16[4,320,128]{2,1,0:T(8,128)(2,1)}, bf16[4,320,128]{2,1,0:T(8,128)(2,1)}, u32[]{:S(2)}, u32[]{:S(2)}) %collective-permute-start.21) | collective-permute-done | bytes 327712 | tf_op jit(solution)/shard_map/ppermute | solution.py:262
  155.6 2.5 %collective-permute-start.23 = (bf16[4,320,128]{2,1,0:T(8,128)(2,1)}, bf16[4,320,128]{2,1,0:T(8,128)(2,1)}, u32[]{:S(2)}, u32[]{:S(2)}) collective-permute-start(bf16[4,320,128]{2,1,0:T(8,128)(2,1)} %collective-permute-done.21.refs_5_), channel_id=1, source_target_pairs={{0,8},{8,16},{16,24},{24,28},{28,20},{20,12},{12,4},{4,0},{1,9},{9... | collective-permute-start | bytes 983048 | tf_op jit(solution)/shard_map/ppermute | solution.py:262
  158.1 4.4 %collective-permute-done.16.refs_7_ = bf16[4,320,128]{2,1,0:T(8,128)(2,1)} collective-permute-done((bf16[4,320,128]{2,1,0:T(8,128)(2,1)}, bf16[4,320,128]{2,1,0:T(8,128)(2,1)}, u32[]{:S(2)}, u32[]{:S(2)}) %collective-permute-start.16) | collective-permute-done | bytes 327712 | tf_op jit(solution)/shard_map/ppermute | solution.py:262
  162.4 1.3 copy-done.6
  163.8 12.7 %shard_map.142 = f32[3,3,160,320]{3,2,1,0:T(8,128)} custom-call(s32[8]{0:T(128)S(1)} %broadcast_multiply_fusion.starts_ref, bf16[4,8,1,160,128]{4,3,2,1,0:T(8,128)(2,1)S(1)} %bitcast.60, bf16[4,320,128]{2,1,0:T(8,128)(2,1)S(1)} %multiply_convert_fusion.refs_0_, bf16[4,320,128]{2,1,0:T(8,128)(2,1)} %collective-permute-done.10.refs_1_, ...), custom_call_target="tpu_custom_call" | custom-call | flops 3774873600 | bytes 5775360 | tf_op jit(solution)/shard_map/pallas_call | solution.py:232
  176.4 0.1 dynamic-slice_bitcast_fusion.2
  176.6 0.8 collective-permute-start.8
  177.4 0.2 collective-permute-start.7
  177.6 0.5 copy-done.3
  178.1 8.0 %shard_map.141 = bf16[4,320,128]{2,1,0:T(8,128)(2,1)} custom-call(bf16[6,1280,128]{2,1,0:T(8,128)(2,1)S(1)} %copy-done.3, bf16[3,3,320,1280]{3,2,1,0:T(8,128)(2,1)} %bitcast.66, bf16[4,320,128]{2,1,0:T(8,128)(2,1)S(1)} %bitcast.59), custom_call_target="tpu_custom_call" | custom-call | flops 3774873600 | bytes 9338880 | tf_op jit(solution)/shard_map/pallas_call | solution.py:78
  186.1 6.0 %collective-permute-done.8 = bf16[4,320,128]{2,1,0:T(8,128)(2,1)S(1)} collective-permute-done((bf16[4,320,128]{2,1,0:T(8,128)(2,1)S(1)}, bf16[4,320,128]{2,1,0:T(8,128)(2,1)S(1)}, u32[]{:S(2)}, u32[]{:S(2)}) %collective-permute-start.8) | collective-permute-done | bytes 327712 | tf_op jit(solution)/shard_map/ppermute | solution.py:300
  192.1 0.8 collective-permute-done.7
  192.9 1.2 fusion.14
  194.1 1.3 copy-done.7
  195.4 12.7 %shard_map.143 = f32[3,3,160,320]{3,2,1,0:T(8,128)} custom-call(s32[8]{0:T(128)S(1)} %broadcast_multiply_fusion.starts_ref, bf16[4,8,1,160,128]{4,3,2,1,0:T(8,128)(2,1)S(1)} %bitcast.61, bf16[4,320,128]{2,1,0:T(8,128)(2,1)S(1)} %bitcast.58, bf16[4,320,128]{2,1,0:T(8,128)(2,1)} %collective-permute-done.17.refs_1_, ...), custom_call_target="tpu_custom_call" | custom-call | flops 3774873600 | bytes 5775360 | tf_op jit(solution)/shard_map/pallas_call | solution.py:232
  (57 shorter events, 0.7 us)
Async XLA Ops:
  7.2 11.0 %copy-start = (f32[1000,320]{0,1:T(8,128)S(1)}, f32[1000,320]{0,1:T(8,128)}, u32[]{:S(2)}) copy-start(f32[1000,320]{0,1:T(8,128)} %param.16) | copy-start | bytes 3840004
  7.2 28.1 %all-gather.7.cloned.1.call-start = ((), (), s32[]{:S(2)}) async-start(), calls=%async_computation.2 | async-start | bytes 2457600 | tf_op jit(solution)/shard_map/all_gather | solution.py:347
  8.4 2.2 %copy-start.1 = (bf16[4,128,320]{1,2,0:T(8,128)(2,1)S(1)}, bf16[4,128,320]{1,2,0:T(8,128)(2,1)}, u32[]{:S(2)}) copy-start(bf16[4,128,320]{1,2,0:T(8,128)(2,1)} %param.18) | copy-start | bytes 983044
  8.5 9.0 %copy-start.9 = (bf16[2,128,320]{1,2,0:T(8,128)(2,1)S(1)}, bf16[2,128,320]{1,2,0:T(8,128)(2,1)}, u32[]{:S(2)}) copy-start(bf16[2,128,320]{1,2,0:T(8,128)(2,1)} %param.13) | copy-start | bytes 491524
  10.5 86.8 %all-gather.9.cloned.1.call-start = ((), (), s32[]{:S(2)}) async-start(), calls=%async_computation.3 | async-start | bytes 2457600 | tf_op jit(solution)/shard_map/all_gather | solution.py:368
  10.6 7.8 %collective-permute-start.1 = (bf16[1,320,128]{2,1,0:T(8,128)(2,1)S(1)}, bf16[1,320,128]{2,1,0:T(8,128)(2,1)S(1)}, u32[]{:S(2)}, u32[]{:S(2)}) collective-permute-start(bf16[1,320,128]{2,1,0:T(8,128)(2,1)S(1)} %get-tuple-element.43), channel_id=1, source_target_pairs={{4,0},{8,4},{12,8},{16,12},{20,16},{24,20},{28,24},{5,1},{9,5},{13... | collective-permute-start | bytes 245768 | tf_op jit(solution)/shard_map/ppermute | solution.py:289
  11.9 8.1 %collective-permute-start = (bf16[1,320,128]{2,1,0:T(8,128)(2,1)S(1)}, bf16[1,320,128]{2,1,0:T(8,128)(2,1)S(1)}, u32[]{:S(2)}, u32[]{:S(2)}) collective-permute-start(bf16[1,320,128]{2,1,0:T(8,128)(2,1)S(1)} %get-tuple-element.42), channel_id=1, source_target_pairs={{0,4},{4,8},{8,12},{12,16},{16,20},{20,24},{24,28},{1,5},{5,9},{9,... | collective-permute-start | bytes 245768 | tf_op jit(solution)/shard_map/ppermute | solution.py:288
  35.4 1.6 copy-start.4
  45.0 0.8 copy-start.5
  45.9 1.3 slice-start.1
  47.9 16.3 %all-to-all-start = ((bf16[8,1,160,128]{3,2,1,0:T(8,128)(2,1)}), bf16[8,1,160,128]{3,2,1,0:T(8,128)(2,1)}, u32[]{:S(2)}, u32[]{:S(2)}) async-start(bf16[8,1,160,128]{3,2,1,0:T(8,128)(2,1)} %bitcast.20), calls=%async_computation | async-start | bytes 655360 | tf_op jit(solution)/shard_map/all_to_all | solution.py:316
  53.5 109.0 %all-gather.11.cloned.1.call-start = ((), (), s32[]{:S(2)}) async-start(), calls=%async_computation.4 | async-start | bytes 1638400 | tf_op jit(solution)/shard_map/all_gather | solution.py:317
  54.5 15.5 %collective-permute-start.4 = (bf16[4,320,128]{2,1,0:T(8,128)(2,1)}, bf16[4,320,128]{2,1,0:T(8,128)(2,1)S(1)}, u32[]{:S(2)}, u32[]{:S(2)}) collective-permute-start(bf16[4,320,128]{2,1,0:T(8,128)(2,1)} %get-tuple-element.37), channel_id=1, source_target_pairs={{0,3},{1,0},{2,1},{3,2},{4,7},{5,4},{6,5},{7,6},{8,11},{9,8},{10,9... | collective-permute-start | bytes 983048 | tf_op jit(solution)/shard_map/ppermute | solution.py:300
  54.7 25.8 %collective-permute-start.3 = (bf16[4,320,128]{2,1,0:T(8,128)(2,1)}, bf16[4,320,128]{2,1,0:T(8,128)(2,1)S(1)}, u32[]{:S(2)}, u32[]{:S(2)}) collective-permute-start(bf16[4,320,128]{2,1,0:T(8,128)(2,1)} %get-tuple-element.38), channel_id=1, source_target_pairs={{0,2},{1,3},{2,0},{3,1},{4,6},{5,7},{6,4},{7,5},{8,10},{9,11},{10,... | collective-permute-start | bytes 983048 | tf_op jit(solution)/shard_map/ppermute | solution.py:300
  56.1 24.3 %collective-permute-start.2 = (bf16[4,320,128]{2,1,0:T(8,128)(2,1)}, bf16[4,320,128]{2,1,0:T(8,128)(2,1)S(1)}, u32[]{:S(2)}, u32[]{:S(2)}) collective-permute-start(bf16[4,320,128]{2,1,0:T(8,128)(2,1)} %get-tuple-element.36), channel_id=1, source_target_pairs={{0,1},{1,2},{2,3},{3,0},{4,5},{5,6},{6,7},{7,4},{8,9},{9,10},{10,1... | collective-permute-start | bytes 983048 | tf_op jit(solution)/shard_map/ppermute | solution.py:300
  81.7 6.3 %collective-permute-start.6 = (bf16[1,320,128]{2,1,0:T(8,128)(2,1)S(1)}, bf16[1,320,128]{2,1,0:T(8,128)(2,1)S(1)}, u32[]{:S(2)}, u32[]{:S(2)}) collective-permute-start(bf16[1,320,128]{2,1,0:T(8,128)(2,1)S(1)} %get-tuple-element.41), channel_id=1, source_target_pairs={{4,0},{8,4},{12,8},{16,12},{20,16},{24,20},{28,24},{5,1},{9,5},{13... | collective-permute-start | bytes 245768 | tf_op jit(solution)/shard_map/ppermute | solution.py:289
  83.0 6.6 %collective-permute-start.5 = (bf16[1,320,128]{2,1,0:T(8,128)(2,1)S(1)}, bf16[1,320,128]{2,1,0:T(8,128)(2,1)S(1)}, u32[]{:S(2)}, u32[]{:S(2)}) collective-permute-start(bf16[1,320,128]{2,1,0:T(8,128)(2,1)S(1)} %get-tuple-element.40), channel_id=1, source_target_pairs={{0,4},{4,8},{8,12},{12,16},{16,20},{20,24},{24,28},{1,5},{5,9},{9,... | collective-permute-start | bytes 245768 | tf_op jit(solution)/shard_map/ppermute | solution.py:288
  97.4 1.3 slice-start
  98.7 38.3 %copy-start.11 = (s32[8]{0:T(128)S(1)}, s32[8]{0:T(128)}, u32[]{:S(2)}) copy-start(s32[8]{0:T(128)} %constant.99.clone) | copy-start | bytes 100
  98.7 38.9 %copy-start.10 = (s32[8]{0:T(128)S(1)}, s32[8]{0:T(128)}, u32[]{:S(2)}) copy-start(s32[8]{0:T(128)} %constant.100.clone) | copy-start | bytes 100
  98.7 52.4 %copy-start.8 = (s32[8]{0:T(128)S(1)}, s32[8]{0:T(128)}, u32[]{:S(2)}) copy-start(s32[8]{0:T(128)} %constant.101.clone) | copy-start | bytes 100
  99.4 23.5 %all-to-all-start.1 = ((bf16[8,1,160,128]{3,2,1,0:T(8,128)(2,1)}), bf16[8,1,160,128]{3,2,1,0:T(8,128)(2,1)}, u32[]{:S(2)}, u32[]{:S(2)}) async-start(bf16[8,1,160,128]{3,2,1,0:T(8,128)(2,1)} %bitcast.62), calls=%async_computation.1 | async-start | bytes 655360 | tf_op jit(solution)/shard_map/all_to_all | solution.py:316
  106.7 87.4 %all-gather.13.cloned.1.call-start = ((), (), s32[]{:S(2)}) async-start(), calls=%async_computation.5 | async-start | bytes 1638400 | tf_op jit(solution)/shard_map/all_gather | solution.py:317
  106.8 13.6 %collective-permute-start.10 = (bf16[4,320,128]{2,1,0:T(8,128)(2,1)S(1)}, bf16[4,320,128]{2,1,0:T(8,128)(2,1)}, u32[]{:S(2)}, u32[]{:S(2)}) collective-permute-start(bf16[4,320,128]{2,1,0:T(8,128)(2,1)S(1)} %multiply_convert_fusion.refs_0_), channel_id=1, source_target_pairs={{0,8},{8,16},{16,24},{24,28},{28,20},{20,12},{12,4},{4,0},{1,9},{9... | collective-permute-start | bytes 983048 | tf_op jit(solution)/shard_map/ppermute | solution.py:262
  108.8 18.6 %collective-permute-start.17 = (bf16[4,320,128]{2,1,0:T(8,128)(2,1)S(1)}, bf16[4,320,128]{2,1,0:T(8,128)(2,1)}, u32[]{:S(2)}, u32[]{:S(2)}) collective-permute-start(bf16[4,320,128]{2,1,0:T(8,128)(2,1)S(1)} %bitcast.56), channel_id=1, source_target_pairs={{0,8},{8,16},{16,24},{24,28},{28,20},{20,12},{12,4},{4,0},{1,9},{9... | collective-permute-start | bytes 983048 | tf_op jit(solution)/shard_map/ppermute | solution.py:262
  110.2 19.8 %collective-permute-start.11 = (bf16[4,320,128]{2,1,0:T(8,128)(2,1)S(1)}, bf16[4,320,128]{2,1,0:T(8,128)(2,1)}, u32[]{:S(2)}, u32[]{:S(2)}) collective-permute-start(bf16[4,320,128]{2,1,0:T(8,128)(2,1)S(1)} %multiply_convert_fusion.refs_0_), channel_id=1, source_target_pairs={{8,0},{16,8},{24,16},{28,24},{20,28},{12,20},{4,12},{0,4},{9,1},{1... | collective-permute-start | bytes 983048 | tf_op jit(solution)/shard_map/ppermute | solution.py:265
  120.4 14.1 %collective-permute-start.12 = (bf16[4,320,128]{2,1,0:T(8,128)(2,1)}, bf16[4,320,128]{2,1,0:T(8,128)(2,1)}, u32[]{:S(2)}, u32[]{:S(2)}) collective-permute-start(bf16[4,320,128]{2,1,0:T(8,128)(2,1)} %collective-permute-done.10.refs_1_), channel_id=1, source_target_pairs={{0,8},{8,16},{16,24},{24,28},{28,20},{20,12},{12,4},{4,0},{1,9},{9... | collective-permute-start | bytes 983048 | tf_op jit(solution)/shard_map/ppermute | solution.py:262
  123.0 15.3 %collective-permute-start.18 = (bf16[4,320,128]{2,1,0:T(8,128)(2,1)S(1)}, bf16[4,320,128]{2,1,0:T(8,128)(2,1)}, u32[]{:S(2)}, u32[]{:S(2)}) collective-permute-start(bf16[4,320,128]{2,1,0:T(8,128)(2,1)S(1)} %bitcast.57), channel_id=1, source_target_pairs={{8,0},{16,8},{24,16},{28,24},{20,28},{12,20},{4,12},{0,4},{9,1},{1... | collective-permute-start | bytes 983048 | tf_op jit(solution)/shard_map/ppermute | solution.py:265
  127.4 14.1 %collective-permute-start.19 = (bf16[4,320,128]{2,1,0:T(8,128)(2,1)}, bf16[4,320,128]{2,1,0:T(8,128)(2,1)}, u32[]{:S(2)}, u32[]{:S(2)}) collective-permute-start(bf16[4,320,128]{2,1,0:T(8,128)(2,1)} %collective-permute-done.17.refs_1_), channel_id=1, source_target_pairs={{0,8},{8,16},{16,24},{24,28},{28,20},{20,12},{12,4},{4,0},{1,9},{9... | collective-permute-start | bytes 983048 | tf_op jit(solution)/shard_map/ppermute | solution.py:262
  130.0 14.0 %collective-permute-start.13 = (bf16[4,320,128]{2,1,0:T(8,128)(2,1)}, bf16[4,320,128]{2,1,0:T(8,128)(2,1)}, u32[]{:S(2)}, u32[]{:S(2)}) collective-permute-start(bf16[4,320,128]{2,1,0:T(8,128)(2,1)} %collective-permute-done.11.refs_2_), channel_id=1, source_target_pairs={{8,0},{16,8},{24,16},{28,24},{20,28},{12,20},{4,12},{0,4},{9,1},{1... | collective-permute-start | bytes 983048 | tf_op jit(solution)/shard_map/ppermute | solution.py:265
  134.5 14.0 %collective-permute-start.14 = (bf16[4,320,128]{2,1,0:T(8,128)(2,1)}, bf16[4,320,128]{2,1,0:T(8,128)(2,1)}, u32[]{:S(2)}, u32[]{:S(2)}) collective-permute-start(bf16[4,320,128]{2,1,0:T(8,128)(2,1)} %collective-permute-done.12.refs_3_), channel_id=1, source_target_pairs={{0,8},{8,16},{16,24},{24,28},{28,20},{20,12},{12,4},{4,0},{1,9},{9... | collective-permute-start | bytes 983048 | tf_op jit(solution)/shard_map/ppermute | solution.py:262
  138.3 13.4 %collective-permute-start.20 = (bf16[4,320,128]{2,1,0:T(8,128)(2,1)}, bf16[4,320,128]{2,1,0:T(8,128)(2,1)}, u32[]{:S(2)}, u32[]{:S(2)}) collective-permute-start(bf16[4,320,128]{2,1,0:T(8,128)(2,1)} %collective-permute-done.18.refs_2_), channel_id=1, source_target_pairs={{8,0},{16,8},{24,16},{28,24},{20,28},{12,20},{4,12},{0,4},{9,1},{1... | collective-permute-start | bytes 983048 | tf_op jit(solution)/shard_map/ppermute | solution.py:265
  141.6 14.0 %collective-permute-start.21 = (bf16[4,320,128]{2,1,0:T(8,128)(2,1)}, bf16[4,320,128]{2,1,0:T(8,128)(2,1)}, u32[]{:S(2)}, u32[]{:S(2)}) collective-permute-start(bf16[4,320,128]{2,1,0:T(8,128)(2,1)} %collective-permute-done.19.refs_3_), channel_id=1, source_target_pairs={{0,8},{8,16},{16,24},{24,28},{28,20},{20,12},{12,4},{4,0},{1,9},{9... | collective-permute-start | bytes 983048 | tf_op jit(solution)/shard_map/ppermute | solution.py:262
  144.0 14.0 %collective-permute-start.15 = (bf16[4,320,128]{2,1,0:T(8,128)(2,1)}, bf16[4,320,128]{2,1,0:T(8,128)(2,1)}, u32[]{:S(2)}, u32[]{:S(2)}) collective-permute-start(bf16[4,320,128]{2,1,0:T(8,128)(2,1)} %collective-permute-done.13.refs_4_), channel_id=1, source_target_pairs={{8,0},{16,8},{24,16},{28,24},{20,28},{12,20},{4,12},{0,4},{9,1},{1... | collective-permute-start | bytes 983048 | tf_op jit(solution)/shard_map/ppermute | solution.py:265
  148.6 13.9 %collective-permute-start.16 = (bf16[4,320,128]{2,1,0:T(8,128)(2,1)}, bf16[4,320,128]{2,1,0:T(8,128)(2,1)}, u32[]{:S(2)}, u32[]{:S(2)}) collective-permute-start(bf16[4,320,128]{2,1,0:T(8,128)(2,1)} %collective-permute-done.14.refs_5_), channel_id=1, source_target_pairs={{0,8},{8,16},{16,24},{24,28},{28,20},{20,12},{12,4},{4,0},{1,9},{9... | collective-permute-start | bytes 983048 | tf_op jit(solution)/shard_map/ppermute | solution.py:262
  151.7 42.4 %collective-permute-start.22 = (bf16[4,320,128]{2,1,0:T(8,128)(2,1)}, bf16[4,320,128]{2,1,0:T(8,128)(2,1)}, u32[]{:S(2)}, u32[]{:S(2)}) collective-permute-start(bf16[4,320,128]{2,1,0:T(8,128)(2,1)} %collective-permute-done.20.refs_4_), channel_id=1, source_target_pairs={{8,0},{16,8},{24,16},{28,24},{20,28},{12,20},{4,12},{0,4},{9,1},{1... | collective-permute-start | bytes 983048 | tf_op jit(solution)/shard_map/ppermute | solution.py:265
  155.6 38.5 %collective-permute-start.23 = (bf16[4,320,128]{2,1,0:T(8,128)(2,1)}, bf16[4,320,128]{2,1,0:T(8,128)(2,1)}, u32[]{:S(2)}, u32[]{:S(2)}) collective-permute-start(bf16[4,320,128]{2,1,0:T(8,128)(2,1)} %collective-permute-done.21.refs_5_), channel_id=1, source_target_pairs={{0,8},{8,16},{16,24},{24,28},{28,20},{20,12},{12,4},{4,0},{1,9},{9... | collective-permute-start | bytes 983048 | tf_op jit(solution)/shard_map/ppermute | solution.py:262
  162.4 1.3 copy-start.6
  176.4 1.1 copy-start.2
  176.4 1.7 copy-start.3
  176.5 9.6 %collective-permute-start.9 = (bf16[4,320,128]{2,1,0:T(8,128)(2,1)S(1)}, bf16[4,320,128]{2,1,0:T(8,128)(2,1)S(1)}, u32[]{:S(2)}, u32[]{:S(2)}) collective-permute-start(bf16[4,320,128]{2,1,0:T(8,128)(2,1)S(1)} %get-tuple-element.33), channel_id=1, source_target_pairs={{0,3},{1,0},{2,1},{3,2},{4,7},{5,4},{6,5},{7,6},{8,11},{9,8},{10,9... | collective-permute-start | bytes 983048 | tf_op jit(solution)/shard_map/ppermute | solution.py:300
  176.6 15.5 %collective-permute-start.8 = (bf16[4,320,128]{2,1,0:T(8,128)(2,1)S(1)}, bf16[4,320,128]{2,1,0:T(8,128)(2,1)S(1)}, u32[]{:S(2)}, u32[]{:S(2)}) collective-permute-start(bf16[4,320,128]{2,1,0:T(8,128)(2,1)S(1)} %get-tuple-element.34), channel_id=1, source_target_pairs={{0,2},{1,3},{2,0},{3,1},{4,6},{5,7},{6,4},{7,5},{8,10},{9,11},{10,... | collective-permute-start | bytes 983048 | tf_op jit(solution)/shard_map/ppermute | solution.py:300
  177.4 15.5 %collective-permute-start.7 = (bf16[4,320,128]{2,1,0:T(8,128)(2,1)S(1)}, bf16[4,320,128]{2,1,0:T(8,128)(2,1)S(1)}, u32[]{:S(2)}, u32[]{:S(2)}) collective-permute-start(bf16[4,320,128]{2,1,0:T(8,128)(2,1)S(1)} %get-tuple-element.32), channel_id=1, source_target_pairs={{0,1},{1,2},{2,3},{3,0},{4,5},{5,6},{6,7},{7,4},{8,9},{9,10},{10,1... | collective-permute-start | bytes 983048 | tf_op jit(solution)/shard_map/ppermute | solution.py:300
  194.1 1.3 copy-start.7
Sparse Core Ops, SparseCore 0:
  10.7 24.5 all-gather.6
  46.0 30.6 all-gather.8
  78.2 17.9 all-gather.10
  123.1 18.6 all-gather.12
